TPU v7x, 768 devices: a whole 4x8x12 slice. The times are simulated.
768 devices in a mesh: ext: 192 (over x_lo, z, y), pair: 4 (over x_hi, core).
Axes of the slice: x: 4 (x_hi: 2, x_lo: 2; x = x_hi * 2 + x_lo), y: 8, z: 12, core: 2. Of those that a mesh axis runs over, the one named last changes fastest.
Arguments:
- core_coef: bfloat16 [1536, 3072], P('ext', 'pair'), may hold values from -6 to 6
- dest_rows: int32 [192, 1536], P('ext'), may hold values from 0 to 255
- block_ids: int32 [192, 1536], P('ext'), may hold values from 0 to 1
- bin_offsets: int32 [192, 192], P('ext'), may hold values from 1 to 8, as said below
- couplings: bfloat16 [2, 3072, 3072], P(None, 'pair'), may hold values from -0.109375 to 0.109375
- energy_gap: float32 [49152, 3072], P('ext', 'pair'), may hold values from 0.5 to 5
Outputs:
- numerators: float32 [49152, 3072], P('ext', 'pair')
- energies: float32 [49152, 3072], P('ext', 'pair')
Inputs may be any that keep to these rules, and one draw needn't show every extreme that they name: bin_offsets[d, d] = 8 for every d.
All inputs are finite; a program needn't handle non-finite values.
Results may differ from a plain program's by a relative error of at most 0.0033.
Values may be sent and summed in bfloat16 or wider, within the bound.
No kernel may reach another device: no remote copies, remote signals or barrier semaphores. Data moves between devices by JAX's collectives and lax.ppermute only.
A program may use at most 64 MiB of HBM per device.

v0:
```python
import jax
import jax.numpy as jnp
from jax import lax
from jax.sharding import PartitionSpec as P


def shards(core_coef, dest_rows, block_ids, bin_offsets, couplings, energy_gap):
    pair_idx = lax.axis_index("pair")
    group_rows = core_coef.shape[0]
    col_width = core_coef.shape[1]
    tile_rows = energy_gap.shape[0]
    block_count = couplings.shape[0]
    group_count = bin_offsets.shape[1]
    string_count = dest_rows.shape[1]
    strings = jnp.arange(string_count, dtype=jnp.int32)
    source_of = strings // group_rows
    within = strings % group_rows
    group_ids = jnp.arange(group_count, dtype=jnp.int32)
    cut_for = jnp.sum(
        jnp.where(source_of[:, None] == group_ids[None, :], bin_offsets[0][None, :], 0), axis=1
    )
    target = jnp.where(within < cut_for, block_ids[0] * tile_rows + dest_rows[0], -1)
    slot_ids = jnp.arange(block_count * tile_rows, dtype=jnp.int32)
    onehot = (slot_ids[:, None] == target[None, :]).astype(jnp.bfloat16)
    summed = jnp.dot(
        onehot,
        lax.all_gather(core_coef, "ext", axis=0, tiled=True),
        preferred_element_type=jnp.float32,
    )
    gathered = summed.astype(jnp.bfloat16).reshape(block_count, tile_rows, col_width)
    partial_value = jnp.einsum(
        "qtb,qbc->tc", gathered, couplings, preferred_element_type=jnp.float32
    )
    summed_all = lax.psum(partial_value, "pair")
    numerators = lax.dynamic_slice_in_dim(summed_all, pair_idx * col_width, col_width, 1)
    energies = -(numerators * numerators) / energy_gap
    return (numerators, energies)


def solution(mesh):
    in_specs = (
        P("ext", "pair"),
        P("ext", None),
        P("ext", None),
        P("ext", None),
        P(None, "pair", None),
        P("ext", "pair"),
    )
    out_specs = (P("ext", "pair"), P("ext", "pair"))
    return jax.shard_map(shards, mesh=mesh, in_specs=in_specs, out_specs=out_specs, check_vma=False)
```

profile of v0, /device:TPU:1, one launch (start us, length us, event | category | flops | bytes accessed | tf_op | source)
XLA Modules:
  0.0 998.3 jit_solution(10158002369241554147)
XLA Ops:
  7.2 0.0 all-gather.2.cloned.1.call-start
  7.2 0.7 all-gather.2.cloned.1.call-update
  7.9 0.0 all-reduce.2.cloned.1.call-start
  8.0 0.9 select_reduce_fusion
  8.9 0.7 fusion.6
  9.6 746.8 %all-gather.2.cloned.1.call-done = bf16[1536,768]{1,0:T(8,128)(2,1)} async-done(((bf16[8,768]{1,0:T(8,128)(2,1)}), bf16[1536,768]{1,0:T(8,128)(2,1)}) %all-gather.2.cloned.1.call-update) | async-done | bytes 2359312 | tf_op jit(solution)/shard_map/all_gather | solution.py:27
  756.4 3.1 fusion.2
  759.6 8.0 convolution_bitcast_fusion
  767.6 0.0 copy-start
  767.6 0.0 all-reduce.2.cloned.1.call-update
  767.6 221.5 %all-reduce.2.cloned.1.call-done = f32[256,3072]{1,0:T(8,128)} async-done(((f32[256,3072]{1,0:T(8,128)}), f32[256,3072]{1,0:T(8,128)}) %all-reduce.2.cloned.1.call-update) | async-done | bytes 3145744 | tf_op jit(solution)/shard_map/psum | solution.py:34
  989.1 0.0 copy-done
  989.1 2.4 negate_divide_fusion
  (1 shorter events, 0.0 us)
Async XLA Ops:
  7.2 749.3 %all-gather.2.cloned.1.call-start = ((), (), s32[]{:S(2)}) async-start(), calls=%async_computation | async-start | bytes 2371584 | tf_op jit(solution)/shard_map/all_gather | solution.py:27
  7.9 981.2 %all-reduce.2.cloned.1.call-start = ((), (), s32[]{:S(2)}) async-start(), calls=%async_computation.1 | async-start | bytes 6291456 | tf_op jit(solution)/shard_map/psum | solution.py:34
  767.6 221.5 %copy-start = (f32[256,768]{1,0:T(8,128)S(1)}, f32[256,768]{1,0:T(8,128)}, u32[]{:S(2)}) copy-start(f32[256,768]{1,0:T(8,128)} %param.11) | copy-start | bytes 2359300
Sparse Core Ops, SparseCore 0:
  10.4 746.0 all-gather.1
  767.7 221.3 all-reduce.1
where the time goes:
time: 999 us; the launch traced here: 998 us
  waiting for transfers between devices  969 us (97%)
  between operations  14.1 us (1%)
  matrix products  11.1 us (1%)
    all_gather x1, waiting for transfers between devices, shards(): lax.all_gather(core_coef, 'ext', axis=0, tiled=True)  747 us
    psum x1, waiting for transfers between devices, shards(): summed_all = lax.psum(partial_value, 'pair')  222 us
  transfers between devices with their start and end apart: 2, of which 2 were waited for; matrix products, arithmetic and copies ran while one was open for 0% of the time, Pallas kernels for 0%

commit v1 on v0

v1 whole, which is shorter than its diff:
```python
import jax
import jax.numpy as jnp
from jax import lax
from jax.sharding import Mesh
from jax.sharding import PartitionSpec as P

NAMES = ("xl", "zh", "zl", "yh", "yl", "xh", "c")
SIZES = (2, 4, 3, 4, 2, 2, 2)
EXT = NAMES[:5]
FAR = ("xl", "zh", "yh")
NEAR = ((1, 1), (-1, -1), (1, 0), (-1, 0), (0, 1))


def shift(dz, dy):
    pairs = []
    for x in range(2):
        for z in range(12):
            for y in range(8):
                pairs.append(((x * 12 + z) * 8 + y, (x * 12 + (z + dz) % 12) * 8 + (y + dy) % 8))
    return pairs


def shards(core_coef, dest_rows, block_ids, bin_offsets, couplings, energy_gap):
    zl, yl = lax.axis_index("zl"), lax.axis_index("yl")
    xh, c = lax.axis_index("xh"), lax.axis_index("c")
    group_rows, width = core_coef.shape
    tile_rows = energy_gap.shape[0]
    spread = jnp.broadcast_to(core_coef[None], (32, group_rows, width))
    own = lax.all_to_all(spread, FAR, 0, 0, tiled=True).reshape(256, width)
    pieces = [own] + [lax.ppermute(own, EXT, shift(*at)) for at in NEAR]

    within = jnp.arange(8, dtype=jnp.int32)
    target = jnp.where(
        within[None, :] < bin_offsets[0][:, None],
        block_ids[0].reshape(192, 8) * tile_rows + dest_rows[0].reshape(192, 8),
        -1,
    )
    target = target.reshape(2, 4, 3, 4, 2, 8).transpose(2, 4, 0, 1, 3, 5).reshape(3, 2, 256)
    slots = jnp.arange(2 * tile_rows, dtype=jnp.int32)
    summed = jnp.zeros((2 * tile_rows, width), jnp.float32)
    for (dz, dy), piece in zip(((0, 0),) + NEAR, pieces):
        row = target[(zl - dz) % 3, (yl - dy) % 2]
        onehot = (slots[:, None] == row[None, :]).astype(jnp.bfloat16)
        summed = summed + jnp.dot(onehot, piece, preferred_element_type=jnp.float32)
    gathered = summed.astype(jnp.bfloat16).reshape(2, tile_rows, width)

    partial = jnp.einsum("qtb,qbc->tc", gathered, couplings, preferred_element_type=jnp.float32)
    swap = [(0, 1), (1, 0)]

    def columns(h, k):
        return lax.dynamic_slice_in_dim(partial, (h * 2 + k) * width, width, 1)

    far_in = lax.ppermute(columns(1 - xh, 1 - c).astype(jnp.bfloat16), "c", swap)
    far = (columns(1 - xh, c) + far_in.astype(jnp.float32)).astype(jnp.bfloat16)
    far = lax.ppermute(far, "xh", swap)
    near_in = lax.ppermute(columns(xh, 1 - c).astype(jnp.bfloat16), "c", swap)
    numerators = columns(xh, c) + near_in.astype(jnp.float32) + far.astype(jnp.float32)
    energies = -(numerators * numerators) / energy_gap
    return (numerators, energies)


def solution(mesh):
    fine = Mesh(mesh.devices.reshape(SIZES), NAMES)
    ext, pair = EXT, NAMES[5:]
    in_specs = (
        P(ext, pair),
        P(ext, None),
        P(ext, None),
        P(ext, None),
        P(None, pair, None),
        P(ext, pair),
    )
    out_specs = (P(ext, pair), P(ext, pair))
    return jax.shard_map(shards, mesh=fine, in_specs=in_specs, out_specs=out_specs, check_vma=False)
```

time: 999 us -> 104 us (0.10)
  waiting for transfers between devices: 969 us -> 29.4 us
  starting transfers between devices: 0.08 us -> 55.1 us
  between operations: 14.1 us -> 0.98 us
    all_gather x1 -> x0, waiting for transfers between devices: 747 us -> none  [shards(): lax.all_gather(core_coef, 'ext', axis=0, tiled=True)]
    psum x1 -> x0, waiting for transfers between devices: 222 us -> none  [shards(): summed_all = lax.psum(partial_value, 'pair')]
    ppermute x0 -> x8, starting transfers between devices: none -> 33.5 us  [the longest x5 22.6 us: shards(): pieces = [own] + [lax.ppermute(own, EXT, shift(*at)) for at in NEAR]]
    all_to_all x0 -> x1, starting transfers between devices: none -> 21.6 us  [shards(): own = lax.all_to_all(spread, FAR, 0, 0, tiled=True).reshape(256, width)]
    ppermute x0 -> x8, waiting for transfers between devices: none -> 17.5 us  [the longest x1 9.53 us: shards(): far = lax.ppermute(far, 'xh', swap)]
    all_to_all x0 -> x1, waiting for transfers between devices: none -> 11.9 us  [shards(): own = lax.all_to_all(spread, FAR, 0, 0, tiled=True).reshape(256, width)]
  transfers between devices with their start and end apart: 2 -> 9, of which waited for: 2 -> 4; matrix products, arithmetic and copies ran while one was open for 0% -> 7% of each run, Pallas kernels for 0% -> 0%
where the time goes in v1:
time: 104 us
  starting transfers between devices  55.1 us (53%)
  waiting for transfers between devices  29.4 us (28%)
  other arithmetic  6.67 us (6%)
  local copies, waits for them, and re-layouts  6.45 us (6%)
  matrix products  5.04 us (5%)
    ppermute x5, starting transfers between devices, shards(): pieces = [own] + [lax.ppermute(own, EXT, shift(*at)) for at in NEAR]  22.6 us
    all_to_all x1, starting transfers between devices, shards(): own = lax.all_to_all(spread, FAR, 0, 0, tiled=True).reshape(256, width)  21.6 us
    all_to_all x1, waiting for transfers between devices, shards(): own = lax.all_to_all(spread, FAR, 0, 0, tiled=True).reshape(256, width)  11.9 us
    ppermute x1, waiting for transfers between devices, shards(): far = lax.ppermute(far, 'xh', swap)  9.53 us
    ppermute x5, waiting for transfers between devices, shards(): pieces = [own] + [lax.ppermute(own, EXT, shift(*at)) for at in NEAR]  7.98 us
    ppermute x1, starting transfers between devices, shards(): lax.ppermute(columns(1 - xh, 1 - c).astype(jnp.bfloat16), 'c', swap)  4.61 us
    ppermute x1, starting transfers between devices, shards(): far = lax.ppermute(far, 'xh', swap)  4.35 us
    unnamed x3, local copies, waits for them, and re-layouts  3.23 us
  transfers between devices with their start and end apart: 9, of which 4 were waited for; matrix products, arithmetic and copies ran while one was open for 7% of the time, Pallas kernels for 0%

profile of v1, /device:TPU:1, one launch (start us, length us, event | category | flops | bytes accessed | tf_op | source)
XLA Modules:
  0.0 103.7 jit_solution(17008727598068911199)
XLA Ops:
  0.6 1.5 %broadcast_in_dim.7 = bf16[32,8,768]{2,1,0:T(8,128)(2,1)} broadcast(bf16[8,768]{1,0:T(8,128)(2,1)} %param.6), dimensions={1,2} | broadcast | bytes 405504 | tf_op jit(solution)/shard_map/broadcast_in_dim | solution.py:28
  2.1 21.6 %all-to-all-start = ((bf16[32,8,768]{2,1,0:T(8,128)(2,1)}), bf16[32,8,768]{2,1,0:T(8,128)(2,1)S(1)}, u32[]{:S(2)}, u32[]{:S(2)}) async-start(bf16[32,8,768]{2,1,0:T(8,128)(2,1)} %broadcast_in_dim.7), calls=%async_computation | async-start | bytes 786432 | tf_op jit(solution)/shard_map/all_to_all | solution.py:29
  23.7 0.7 add_reduce_fusion
  24.5 0.2 add.109
  24.7 0.5 broadcast.17
  25.2 1.3 %reduce.5 = s32[192]{0:T(256)S(1)} reduce(s32[1,192]{1,0:T(1,128)} %param.9, s32[]{:T(128)} %broadcast.17), dimensions={0}, to_apply=%param.9.reduce_sub_computation.3 | reduce | bytes 1540 | tf_op args[3]
  26.5 0.2 lt.91
  26.7 0.3 copy.8
  27.0 11.9 %all-to-all-done = bf16[32,8,768]{2,1,0:T(8,128)(2,1)S(1)} async-done(((bf16[32,8,768]{2,1,0:T(8,128)(2,1)}), bf16[32,8,768]{2,1,0:T(8,128)(2,1)S(1)}, u32[]{:S(2)}, u32[]{:S(2)}) %all-to-all-start) | async-done | bytes 393248 | tf_op jit(solution)/shard_map/all_to_all | solution.py:29
  38.9 11.0 %collective-permute-start = (bf16[256,768]{1,0:T(8,128)(2,1)S(1)}, bf16[256,768]{1,0:T(8,128)(2,1)S(1)}, u32[]{:S(2)}, u32[]{:S(2)}) collective-permute-start(bf16[256,768]{1,0:T(8,128)(2,1)S(1)} %bitcast.21), channel_id=1, source_target_pairs={{0,36},{4,40},{8,44},{12,48},{16,52},{20,56},{24,60},{28,32},{32,6... | collective-permute-start | bytes 1179656 | tf_op jit(solution)/shard_map/ppermute | solution.py:30
  49.9 0.1 fusion.12
  50.1 0.1 reshape.35
  50.3 1.9 %collective-permute-start.1 = (bf16[256,768]{1,0:T(8,128)(2,1)S(1)}, bf16[256,768]{1,0:T(8,128)(2,1)S(1)}, u32[]{:S(2)}, u32[]{:S(2)}) collective-permute-start(bf16[256,768]{1,0:T(8,128)(2,1)S(1)} %bitcast.22), channel_id=1, source_target_pairs={{0,380},{4,352},{8,356},{12,360},{16,364},{20,368},{24,372},{28,37... | collective-permute-start | bytes 1179656 | tf_op jit(solution)/shard_map/ppermute | solution.py:30
  52.3 5.4 %collective-permute-start.2 = (bf16[256,768]{1,0:T(8,128)(2,1)S(1)}, bf16[256,768]{1,0:T(8,128)(2,1)S(1)}, u32[]{:S(2)}, u32[]{:S(2)}) collective-permute-start(bf16[256,768]{1,0:T(8,128)(2,1)S(1)} %bitcast.23), channel_id=1, source_target_pairs={{0,32},{4,36},{8,40},{12,44},{16,48},{20,52},{24,56},{28,60},{32,6... | collective-permute-start | bytes 1179656 | tf_op jit(solution)/shard_map/ppermute | solution.py:30
  57.6 2.1 %collective-permute-start.3 = (bf16[256,768]{1,0:T(8,128)(2,1)S(1)}, bf16[256,768]{1,0:T(8,128)(2,1)S(1)}, u32[]{:S(2)}, u32[]{:S(2)}) collective-permute-start(bf16[256,768]{1,0:T(8,128)(2,1)S(1)} %bitcast.24), channel_id=1, source_target_pairs={{0,352},{4,356},{8,360},{12,364},{16,368},{20,372},{24,376},{28,38... | collective-permute-start | bytes 1179656 | tf_op jit(solution)/shard_map/ppermute | solution.py:30
  59.8 2.2 %collective-permute-start.4 = (bf16[256,768]{1,0:T(8,128)(2,1)S(1)}, bf16[256,768]{1,0:T(8,128)(2,1)S(1)}, u32[]{:S(2)}, u32[]{:S(2)}) collective-permute-start(bf16[256,768]{1,0:T(8,128)(2,1)S(1)} %bitcast.25), channel_id=1, source_target_pairs={{0,4},{4,8},{8,12},{12,16},{16,20},{20,24},{24,28},{28,0},{32,36},... | collective-permute-start | bytes 1179656 | tf_op jit(solution)/shard_map/ppermute | solution.py:30
  62.0 0.4 fusion
  62.3 0.0 collective-permute-done
  62.3 0.4 fusion.1
  62.7 0.0 collective-permute-done.1
  62.7 0.4 fusion.2
  63.1 2.6 %collective-permute-done.2 = bf16[256,768]{1,0:T(8,128)(2,1)S(1)} collective-permute-done((bf16[256,768]{1,0:T(8,128)(2,1)S(1)}, bf16[256,768]{1,0:T(8,128)(2,1)S(1)}, u32[]{:S(2)}, u32[]{:S(2)}) %collective-permute-start.2) | collective-permute-done | bytes 393248 | tf_op jit(solution)/shard_map/ppermute | solution.py:30
  65.7 0.4 fusion.3
  66.1 5.4 %collective-permute-done.3 = bf16[256,768]{1,0:T(8,128)(2,1)S(1)} collective-permute-done((bf16[256,768]{1,0:T(8,128)(2,1)S(1)}, bf16[256,768]{1,0:T(8,128)(2,1)S(1)}, u32[]{:S(2)}, u32[]{:S(2)}) %collective-permute-start.3) | collective-permute-done | bytes 393248 | tf_op jit(solution)/shard_map/ppermute | solution.py:30
  71.5 0.0 copy-start
  71.5 0.4 fusion.4
  71.9 0.0 collective-permute-done.4
  71.9 0.6 add_convert_fusion
  72.4 2.7 %copy-done = bf16[2,768,3072]{2,1,0:T(8,128)(2,1)S(1)} copy-done((bf16[2,768,3072]{2,1,0:T(8,128)(2,1)S(1)}, bf16[2,768,3072]{2,1,0:T(8,128)(2,1)}, u32[]{:S(2)}) %copy-start) | copy-done | bytes 9437208
  75.2 2.6 %convolution_bitcast_fusion = f32[256,3072]{1,0:T(8,128)S(1)} fusion(bf16[2,256,768]{2,1,0:T(8,128)(2,1)S(1)} %bitcast.26, bf16[2,768,3072]{2,1,0:T(8,128)(2,1)S(1)} %copy-done), kind=kOutput, calls=%fused_computation | convolution fusion | flops 2415919104 | bytes 13369344 | tf_op jit(solution)/shard_map/qtb,qbc->tc/dot_general | solution.py:47
  77.8 1.0 dynamic-slice_convert_fusion.1
  78.7 4.6 %collective-permute-start.6 = (bf16[256,768]{1,0:T(8,128)(2,1)}, bf16[256,768]{1,0:T(8,128)(2,1)}, u32[]{:S(2)}, u32[]{:S(2)}) collective-permute-start(bf16[256,768]{1,0:T(8,128)(2,1)} %get-tuple-element.5), channel_id=1, source_target_pairs={{0,1},{1,0},{2,3},{3,2},{4,5},{5,4},{6,7},{7,6},{8,9},{9,8},{10,11... | collective-permute-start | bytes 1179656 | tf_op jit(solution)/shard_map/ppermute | solution.py:53
  83.4 1.9 %collective-permute-start.5 = (bf16[256,768]{1,0:T(8,128)(2,1)}, bf16[256,768]{1,0:T(8,128)(2,1)S(1)}, u32[]{:S(2)}, u32[]{:S(2)}) collective-permute-start(bf16[256,768]{1,0:T(8,128)(2,1)} %get-tuple-element.4), channel_id=1, source_target_pairs={{0,1},{1,0},{2,3},{3,2},{4,5},{5,4},{6,7},{7,6},{8,9},{9,8},{10,11... | collective-permute-start | bytes 1179656 | tf_op jit(solution)/shard_map/ppermute | solution.py:56
  85.3 0.0 collective-permute-done.6
  85.3 1.9 %add_convert_fusion.1 = bf16[256,768]{1,0:T(8,128)(2,1)} fusion(bf16[256,768]{1,0:T(8,128)(2,1)} %collective-permute-done.6, f32[256,3072]{1,0:T(8,128)S(1)} %convolution_bitcast_fusion, s32[]{:T(128)S(6)} %select_n.95), kind=kLoop, calls=%fused_computation.4 | loop fusion | flops 589824 | bytes 1572868 | tf_op jit(solution)/shard_map/convert_element_type | solution.py:54
  87.2 4.3 %collective-permute-start.7 = (bf16[256,768]{1,0:T(8,128)(2,1)}, bf16[256,768]{1,0:T(8,128)(2,1)}, u32[]{:S(2)}, u32[]{:S(2)}) collective-permute-start(bf16[256,768]{1,0:T(8,128)(2,1)} %add_convert_fusion.1), channel_id=1, source_target_pairs={{0,2},{2,0},{1,3},{3,1},{4,6},{6,4},{5,7},{7,5},{8,10},{10,8},{9,1... | collective-permute-start | bytes 1179656 | tf_op jit(solution)/shard_map/ppermute | solution.py:55
  91.5 0.0 collective-permute-done.5
  91.5 9.5 %collective-permute-done.7 = bf16[256,768]{1,0:T(8,128)(2,1)} collective-permute-done((bf16[256,768]{1,0:T(8,128)(2,1)}, bf16[256,768]{1,0:T(8,128)(2,1)}, u32[]{:S(2)}, u32[]{:S(2)}) %collective-permute-start.7) | collective-permute-done | bytes 393248 | tf_op jit(solution)/shard_map/ppermute | solution.py:55
  101.1 2.6 %negate_divide_fusion = (f32[256,768]{1,0:T(8,128)}, f32[256,768]{1,0:T(8,128)}) fusion(f32[256,768]{1,0:T(8,128)} %param.11, bf16[256,768]{1,0:T(8,128)(2,1)} %collective-permute-done.7, bf16[256,768]{1,0:T(8,128)(2,1)S(1)} %collective-permute-done.5, f32[256,3072]{1,0:T(8,128)S(1)} %convolution_bitcast_fusion, s32[]{:T(128)S(6)} %select_n.93), kind=kLoop, calls=%fused_computation.2 | loop fusion | flops 1376256 | bytes 3932164 | tf_op jit(solution)/shard_map/div | solution.py:58
  (1 shorter events, 0.0 us)
Async XLA Ops:
  2.1 36.8 %all-to-all-start = ((bf16[32,8,768]{2,1,0:T(8,128)(2,1)}), bf16[32,8,768]{2,1,0:T(8,128)(2,1)S(1)}, u32[]{:S(2)}, u32[]{:S(2)}) async-start(bf16[32,8,768]{2,1,0:T(8,128)(2,1)} %broadcast_in_dim.7), calls=%async_computation | async-start | bytes 786432 | tf_op jit(solution)/shard_map/all_to_all | solution.py:29
  38.9 23.5 %collective-permute-start = (bf16[256,768]{1,0:T(8,128)(2,1)S(1)}, bf16[256,768]{1,0:T(8,128)(2,1)S(1)}, u32[]{:S(2)}, u32[]{:S(2)}) collective-permute-start(bf16[256,768]{1,0:T(8,128)(2,1)S(1)} %bitcast.21), channel_id=1, source_target_pairs={{0,36},{4,40},{8,44},{12,48},{16,52},{20,56},{24,60},{28,32},{32,6... | collective-permute-start | bytes 1179656 | tf_op jit(solution)/shard_map/ppermute | solution.py:30
  50.3 12.4 %collective-permute-start.1 = (bf16[256,768]{1,0:T(8,128)(2,1)S(1)}, bf16[256,768]{1,0:T(8,128)(2,1)S(1)}, u32[]{:S(2)}, u32[]{:S(2)}) collective-permute-start(bf16[256,768]{1,0:T(8,128)(2,1)S(1)} %bitcast.22), channel_id=1, source_target_pairs={{0,380},{4,352},{8,356},{12,360},{16,364},{20,368},{24,372},{28,37... | collective-permute-start | bytes 1179656 | tf_op jit(solution)/shard_map/ppermute | solution.py:30
  52.3 13.5 %collective-permute-start.2 = (bf16[256,768]{1,0:T(8,128)(2,1)S(1)}, bf16[256,768]{1,0:T(8,128)(2,1)S(1)}, u32[]{:S(2)}, u32[]{:S(2)}) collective-permute-start(bf16[256,768]{1,0:T(8,128)(2,1)S(1)} %bitcast.23), channel_id=1, source_target_pairs={{0,32},{4,36},{8,40},{12,44},{16,48},{20,52},{24,56},{28,60},{32,6... | collective-permute-start | bytes 1179656 | tf_op jit(solution)/shard_map/ppermute | solution.py:30
  57.6 13.8 %collective-permute-start.3 = (bf16[256,768]{1,0:T(8,128)(2,1)S(1)}, bf16[256,768]{1,0:T(8,128)(2,1)S(1)}, u32[]{:S(2)}, u32[]{:S(2)}) collective-permute-start(bf16[256,768]{1,0:T(8,128)(2,1)S(1)} %bitcast.24), channel_id=1, source_target_pairs={{0,352},{4,356},{8,360},{12,364},{16,368},{20,372},{24,376},{28,38... | collective-permute-start | bytes 1179656 | tf_op jit(solution)/shard_map/ppermute | solution.py:30
  59.8 12.1 %collective-permute-start.4 = (bf16[256,768]{1,0:T(8,128)(2,1)S(1)}, bf16[256,768]{1,0:T(8,128)(2,1)S(1)}, u32[]{:S(2)}, u32[]{:S(2)}) collective-permute-start(bf16[256,768]{1,0:T(8,128)(2,1)S(1)} %bitcast.25), channel_id=1, source_target_pairs={{0,4},{4,8},{8,12},{12,16},{16,20},{20,24},{24,28},{28,0},{32,36},... | collective-permute-start | bytes 1179656 | tf_op jit(solution)/shard_map/ppermute | solution.py:30
  71.5 3.7 %copy-start = (bf16[2,768,3072]{2,1,0:T(8,128)(2,1)S(1)}, bf16[2,768,3072]{2,1,0:T(8,128)(2,1)}, u32[]{:S(2)}) copy-start(bf16[2,768,3072]{2,1,0:T(8,128)(2,1)} %param.10) | copy-start | bytes 28311556
  78.7 6.6 %collective-permute-start.6 = (bf16[256,768]{1,0:T(8,128)(2,1)}, bf16[256,768]{1,0:T(8,128)(2,1)}, u32[]{:S(2)}, u32[]{:S(2)}) collective-permute-start(bf16[256,768]{1,0:T(8,128)(2,1)} %get-tuple-element.5), channel_id=1, source_target_pairs={{0,1},{1,0},{2,3},{3,2},{4,5},{5,4},{6,7},{7,6},{8,9},{9,8},{10,11... | collective-permute-start | bytes 1179656 | tf_op jit(solution)/shard_map/ppermute | solution.py:53
  83.4 8.2 %collective-permute-start.5 = (bf16[256,768]{1,0:T(8,128)(2,1)}, bf16[256,768]{1,0:T(8,128)(2,1)S(1)}, u32[]{:S(2)}, u32[]{:S(2)}) collective-permute-start(bf16[256,768]{1,0:T(8,128)(2,1)} %get-tuple-element.4), channel_id=1, source_target_pairs={{0,1},{1,0},{2,3},{3,2},{4,5},{5,4},{6,7},{7,6},{8,9},{9,8},{10,11... | collective-permute-start | bytes 1179656 | tf_op jit(solution)/shard_map/ppermute | solution.py:56
  87.2 13.9 %collective-permute-start.7 = (bf16[256,768]{1,0:T(8,128)(2,1)}, bf16[256,768]{1,0:T(8,128)(2,1)}, u32[]{:S(2)}, u32[]{:S(2)}) collective-permute-start(bf16[256,768]{1,0:T(8,128)(2,1)} %add_convert_fusion.1), channel_id=1, source_target_pairs={{0,2},{2,0},{1,3},{3,1},{4,6},{6,4},{5,7},{7,5},{8,10},{10,8},{9,1... | collective-permute-start | bytes 1179656 | tf_op jit(solution)/shard_map/ppermute | solution.py:55

commit v2 on v1

v2 whole, which is shorter than its diff:
```python
import jax
import jax.numpy as jnp
from jax import lax
from jax.sharding import Mesh
from jax.sharding import PartitionSpec as P

NAMES = ("xl", "zh", "zl", "yh", "yl", "xh", "c")
SIZES = (2, 6, 2, 4, 2, 2, 2)
EXT = NAMES[:5]
FAR = ("zh", "yh")
NEAR = ((1, 1), (1, 0), (0, 1))
SWAP = [(0, 1), (1, 0)]


def shift(dx, dz, dy):
    pairs = []
    for x in range(2):
        for z in range(12):
            for y in range(8):
                for k in range(4):
                    s = -1 if k % 2 else 1
                    there = (((x + dx) % 2) * 12 + (z + s * dz) % 12) * 8 + (y + s * dy) % 8
                    pairs.append((((x * 12 + z) * 8 + y) * 4 + k, there * 4 + k))
    return pairs


def shards(core_coef, dest_rows, block_ids, bin_offsets, couplings, energy_gap):
    xl, zl, yl = lax.axis_index("xl"), lax.axis_index("zl"), lax.axis_index("yl")
    xh, c = lax.axis_index("xh"), lax.axis_index("c")
    group_rows, width = core_coef.shape
    tile_rows = energy_gap.shape[0]
    spread = jnp.broadcast_to(core_coef[None], (24, group_rows, width))
    own = lax.all_to_all(spread, FAR, 0, 0, tiled=True).reshape(192, width)
    beside = lax.ppermute(own, NAMES, shift(1, 0, 0))
    pieces = [((0, 0, 0), own)]
    pieces += [((0,) + at, lax.ppermute(own, NAMES, shift(0, *at))) for at in NEAR]
    pieces += [((1, 0, 0), beside)]
    pieces += [((1,) + at, lax.ppermute(beside, NAMES, shift(0, *at))) for at in NEAR]

    within = jnp.arange(8, dtype=jnp.int32)
    target = jnp.where(
        within[None, :] < bin_offsets[0][:, None],
        block_ids[0].reshape(192, 8) * tile_rows + dest_rows[0].reshape(192, 8),
        -1,
    )
    target = target.reshape(2, 6, 2, 4, 2, 8).transpose(0, 2, 4, 1, 3, 5).reshape(2, 2, 2, 192)
    slots = jnp.arange(2 * tile_rows, dtype=jnp.int32)
    summed = jnp.zeros((2 * tile_rows, width), jnp.float32)
    for (dx, dz, dy), piece in pieces:
        row = target[(xl + dx) % 2, (zl + dz) % 2, (yl + dy) % 2]
        onehot = (slots[:, None] == row[None, :]).astype(jnp.bfloat16)
        summed = summed + jnp.dot(onehot, piece, preferred_element_type=jnp.float32)
    gathered = summed.astype(jnp.bfloat16).reshape(2, tile_rows, width)

    def columns(rows, h, k):
        block = lax.dynamic_slice_in_dim(couplings, (h * 2 + k) * width, width, 2)
        return jnp.einsum("qtb,qbc->tc", rows, block, preferred_element_type=jnp.float32)

    far_in = lax.ppermute(columns(gathered, 1 - xh, 1 - c).astype(jnp.bfloat16), "c", SWAP)
    far = (columns(gathered, 1 - xh, c) + far_in.astype(jnp.float32)).astype(jnp.bfloat16)
    far, gathered = lax.optimization_barrier((far, gathered))
    far = lax.ppermute(far, "xh", SWAP)
    near_in = lax.ppermute(columns(gathered, xh, 1 - c).astype(jnp.bfloat16), "c", SWAP)
    numerators = columns(gathered, xh, c) + near_in.astype(jnp.float32) + far.astype(jnp.float32)
    energies = -(numerators * numerators) / energy_gap
    return (numerators, energies)


def solution(mesh):
    fine = Mesh(mesh.devices.reshape(SIZES), NAMES)
    ext, pair = EXT, NAMES[5:]
    in_specs = (
        P(ext, pair),
        P(ext, None),
        P(ext, None),
        P(ext, None),
        P(None, pair, None),
        P(ext, pair),
    )
    out_specs = (P(ext, pair), P(ext, pair))
    return jax.shard_map(shards, mesh=fine, in_specs=in_specs, out_specs=out_specs, check_vma=False)
```

time: 104 us -> 102 us (0.981)
  matrix products: 5.04 us -> 13.1 us
  local copies, waits for them, and re-layouts: 6.45 us -> 2.75 us
  other arithmetic: 6.67 us -> 3.57 us
  waiting for transfers between devices: 29.4 us -> 27.5 us
  starting transfers between devices: 55.1 us -> 53.4 us
    dot_general x1 -> x4, matrix products: 2.6 us -> 9.84 us  [columns(): jnp.einsum('qtb,qbc->tc', rows, block, preferred_element_type=jnp.float32)]
    ppermute x8 -> x10, waiting for transfers between devices: 17.5 us -> 12.3 us  [the longest x1 7.06 us: shards(): far = lax.ppermute(far, 'xh', SWAP)]
    all_to_all x1, waiting for transfers between devices: 11.9 us -> 15.2 us  [shards(): own = lax.all_to_all(spread, FAR, 0, 0, tiled=True).reshape(192, width)]
    unnamed x3, local copies, waits for them, and re-layouts: 3.23 us -> 0.52 us
    convert_element_type x1 -> x0, other arithmetic: 1.86 us -> none  [shards(): far = (columns(1 - xh, c) + far_in.astype(jnp.float32)).astype(jnp.bfloat16)]
    div x1, other arithmetic: 2.62 us -> 1.36 us  [shards(): energies = -(numerators * numerators) / energy_gap]
    all_to_all x1, starting transfers between devices: 21.6 us -> 20.6 us  [shards(): own = lax.all_to_all(spread, FAR, 0, 0, tiled=True).reshape(192, width)]
    dot_general x6 -> x8, matrix products: 2.44 us -> 3.26 us  [shards(): summed = summed + jnp.dot(onehot, piece, preferred_element_type=jnp.float32)]
  transfers between devices with their start and end apart: 9 -> 11, of which waited for: 4 -> 6; matrix products, arithmetic and copies ran while one was open for 7% -> 8% of each run, Pallas kernels for 0% -> 0%
where the time goes in v2:
time: 102 us; the launch traced here: 101 us
  starting transfers between devices  53.4 us (52%)
  waiting for transfers between devices  27.5 us (27%)
  matrix products  13.1 us (13%)
  other arithmetic  3.57 us (4%)
  local copies, waits for them, and re-layouts  2.75 us (3%)
  between operations  1.02 us (1%)
    all_to_all x1, starting transfers between devices, shards(): own = lax.all_to_all(spread, FAR, 0, 0, tiled=True).reshape(192, width)  20.6 us
    all_to_all x1, waiting for transfers between devices, shards(): own = lax.all_to_all(spread, FAR, 0, 0, tiled=True).reshape(192, width)  15.2 us
    ppermute x3, starting transfers between devices, shards(): lax.ppermute(own, NAMES, shift(0, *at))  10.7 us
    dot_general x4, matrix products, columns(): jnp.einsum('qtb,qbc->tc', rows, block, preferred_element_type=jnp.float32)  9.84 us
    ppermute x1, waiting for transfers between devices, shards(): far = lax.ppermute(far, 'xh', SWAP)  7.06 us
    ppermute x3, starting transfers between devices, shards(): lax.ppermute(beside, NAMES, shift(0, *at))  6.3 us
    ppermute x1, starting transfers between devices, shards(): lax.ppermute(columns(gathered, 1 - xh, 1 - c).astype(jnp.bfloat16), 'c',...  6.04 us
    ppermute x1, starting transfers between devices, shards(): far = lax.ppermute(far, 'xh', SWAP)  4.35 us
  transfers between devices with their start and end apart: 11, of which 6 were waited for; matrix products, arithmetic and copies ran while one was open for 8% of the time, Pallas kernels for 0%

profile of v2, /device:TPU:1, one launch (start us, length us, event | category | flops | bytes accessed | tf_op | source)
XLA Modules:
  0.0 101.4 jit_solution(7589957486537721812)
XLA Ops:
  0.6 1.4 %broadcast_in_dim.7 = bf16[24,8,768]{2,1,0:T(8,128)(2,1)} broadcast(bf16[8,768]{1,0:T(8,128)(2,1)} %param.6), dimensions={1,2} | broadcast | bytes 307200 | tf_op jit(solution)/shard_map/broadcast_in_dim | solution.py:32
  2.1 20.6 %all-to-all-start = ((bf16[24,8,768]{2,1,0:T(8,128)(2,1)}), bf16[24,8,768]{2,1,0:T(8,128)(2,1)S(1)}, u32[]{:S(2)}, u32[]{:S(2)}) async-start(bf16[24,8,768]{2,1,0:T(8,128)(2,1)} %broadcast_in_dim.7), calls=%async_computation | async-start | bytes 589824 | tf_op jit(solution)/shard_map/all_to_all | solution.py:33
  22.7 0.7 add_reduce_fusion
  23.4 0.2 add.153
  23.6 0.5 broadcast.20
  24.2 1.3 %reduce.5 = s32[192]{0:T(256)S(1)} reduce(s32[1,192]{1,0:T(1,128)} %param.9, s32[]{:T(128)} %broadcast.20), dimensions={0}, to_apply=%param.9.reduce_sub_computation.3 | reduce | bytes 1540 | tf_op args[3]
  25.5 0.2 lt.127
  25.7 0.3 copy.8
  26.0 0.1 fusion.42
  26.1 0.1 reshape.37
  26.3 15.2 %all-to-all-done = bf16[24,8,768]{2,1,0:T(8,128)(2,1)S(1)} async-done(((bf16[24,8,768]{2,1,0:T(8,128)(2,1)}), bf16[24,8,768]{2,1,0:T(8,128)(2,1)S(1)}, u32[]{:S(2)}, u32[]{:S(2)}) %all-to-all-start) | async-done | bytes 294944 | tf_op jit(solution)/shard_map/all_to_all | solution.py:33
  41.4 3.1 %collective-permute-start.3 = (bf16[192,768]{1,0:T(8,128)(2,1)S(1)}, bf16[192,768]{1,0:T(8,128)(2,1)S(1)}, u32[]{:S(2)}, u32[]{:S(2)}) collective-permute-start(bf16[192,768]{1,0:T(8,128)(2,1)S(1)} %bitcast.43), channel_id=1, source_target_pairs={{0,384},{1,385},{2,386},{3,387},{4,388},{5,389},{6,390},{7,391},{8... | collective-permute-start | bytes 884744 | tf_op jit(solution)/shard_map/ppermute | solution.py:34
  44.6 5.8 %collective-permute-start = (bf16[192,768]{1,0:T(8,128)(2,1)S(1)}, bf16[192,768]{1,0:T(8,128)(2,1)S(1)}, u32[]{:S(2)}, u32[]{:S(2)}) collective-permute-start(bf16[192,768]{1,0:T(8,128)(2,1)S(1)} %bitcast.44), channel_id=1, source_target_pairs={{0,36},{1,381},{2,38},{3,383},{4,40},{5,353},{6,42},{7,355},{8,44}... | collective-permute-start | bytes 884744 | tf_op jit(solution)/shard_map/ppermute | solution.py:36
  50.5 1.9 %collective-permute-start.1 = (bf16[192,768]{1,0:T(8,128)(2,1)S(1)}, bf16[192,768]{1,0:T(8,128)(2,1)S(1)}, u32[]{:S(2)}, u32[]{:S(2)}) collective-permute-start(bf16[192,768]{1,0:T(8,128)(2,1)S(1)} %bitcast.45), channel_id=1, source_target_pairs={{0,32},{1,353},{2,34},{3,355},{4,36},{5,357},{6,38},{7,359},{8,40}... | collective-permute-start | bytes 884744 | tf_op jit(solution)/shard_map/ppermute | solution.py:36
  52.4 3.0 %collective-permute-start.2 = (bf16[192,768]{1,0:T(8,128)(2,1)S(1)}, bf16[192,768]{1,0:T(8,128)(2,1)S(1)}, u32[]{:S(2)}, u32[]{:S(2)}) collective-permute-start(bf16[192,768]{1,0:T(8,128)(2,1)S(1)} %bitcast.46), channel_id=1, source_target_pairs={{0,4},{1,29},{2,6},{3,31},{4,8},{5,1},{6,10},{7,3},{8,12},{9,5},{1... | collective-permute-start | bytes 884744 | tf_op jit(solution)/shard_map/ppermute | solution.py:36
  55.4 0.4 fusion.26
  55.7 0.0 collective-permute-done.3
  55.8 2.2 %collective-permute-start.4 = (bf16[192,768]{1,0:T(8,128)(2,1)S(1)}, bf16[192,768]{1,0:T(8,128)(2,1)S(1)}, u32[]{:S(2)}, u32[]{:S(2)}) collective-permute-start(bf16[192,768]{1,0:T(8,128)(2,1)S(1)} %collective-permute-done.3), channel_id=1, source_target_pairs={{0,36},{1,381},{2,38},{3,383},{4,40},{5,353},{6,42},{7,355},{8,44}... | collective-permute-start | bytes 884744 | tf_op jit(solution)/shard_map/ppermute | solution.py:38
  58.0 2.2 %collective-permute-start.5 = (bf16[192,768]{1,0:T(8,128)(2,1)S(1)}, bf16[192,768]{1,0:T(8,128)(2,1)S(1)}, u32[]{:S(2)}, u32[]{:S(2)}) collective-permute-start(bf16[192,768]{1,0:T(8,128)(2,1)S(1)} %collective-permute-done.3), channel_id=1, source_target_pairs={{0,32},{1,353},{2,34},{3,355},{4,36},{5,357},{6,38},{7,359},{8,40}... | collective-permute-start | bytes 884744 | tf_op jit(solution)/shard_map/ppermute | solution.py:38
  60.2 0.4 fusion.30
  60.5 0.0 collective-permute-done
  60.5 1.9 %collective-permute-start.6 = (bf16[192,768]{1,0:T(8,128)(2,1)S(1)}, bf16[192,768]{1,0:T(8,128)(2,1)S(1)}, u32[]{:S(2)}, u32[]{:S(2)}) collective-permute-start(bf16[192,768]{1,0:T(8,128)(2,1)S(1)} %collective-permute-done.3), channel_id=1, source_target_pairs={{0,4},{1,29},{2,6},{3,31},{4,8},{5,1},{6,10},{7,3},{8,12},{9,5},{1... | collective-permute-start | bytes 884744 | tf_op jit(solution)/shard_map/ppermute | solution.py:38
  62.5 0.4 fusion.27
  62.8 0.0 collective-permute-done.1
  62.9 0.4 fusion.28
  63.2 0.0 collective-permute-done.2
  63.2 0.4 fusion.29
  63.6 0.5 collective-permute-done.4
  64.1 0.4 fusion.31
  64.5 2.2 %collective-permute-done.5 = bf16[192,768]{1,0:T(8,128)(2,1)S(1)} collective-permute-done((bf16[192,768]{1,0:T(8,128)(2,1)S(1)}, bf16[192,768]{1,0:T(8,128)(2,1)S(1)}, u32[]{:S(2)}, u32[]{:S(2)}) %collective-permute-start.5) | collective-permute-done | bytes 294944 | tf_op jit(solution)/shard_map/ppermute | solution.py:38
  66.7 0.4 fusion.32
  67.1 1.2 %collective-permute-done.6 = bf16[192,768]{1,0:T(8,128)(2,1)S(1)} collective-permute-done((bf16[192,768]{1,0:T(8,128)(2,1)S(1)}, bf16[192,768]{1,0:T(8,128)(2,1)S(1)}, u32[]{:S(2)}, u32[]{:S(2)}) %collective-permute-start.6) | collective-permute-done | bytes 294944 | tf_op jit(solution)/shard_map/ppermute | solution.py:38
  68.3 0.7 add_convert_fusion
  69.0 2.4 %fusion.23 = bf16[256,768]{1,0:T(8,128)(2,1)S(1)} fusion(bf16[2,256,768]{2,1,0:T(8,128)(2,1)S(1)} %bitcast.39, bf16[2,768,3072]{2,1,0:T(8,128)(2,1)} %param.10, s32[]{:T(128)S(6)} %select_n.130), kind=kOutput, calls=%fused_computation.14 | convolution fusion | flops 604176384 | bytes 3538948 | tf_op jit(solution)/shard_map/qtb,qbc->tc/dot_general | solution.py:57
  71.5 6.0 %collective-permute-start.7 = (bf16[256,768]{1,0:T(8,128)(2,1)S(1)}, bf16[256,768]{1,0:T(8,128)(2,1)S(1)}, u32[]{:S(2)}, u32[]{:S(2)}) collective-permute-start(bf16[256,768]{1,0:T(8,128)(2,1)S(1)} %fusion.23), channel_id=1, source_target_pairs={{0,1},{1,0},{2,3},{3,2},{4,5},{5,4},{6,7},{7,6},{8,9},{9,8},{10,11... | collective-permute-start | bytes 1179656 | tf_op jit(solution)/shard_map/ppermute | solution.py:59
  77.5 1.3 %collective-permute-done.7 = bf16[256,768]{1,0:T(8,128)(2,1)S(1)} collective-permute-done((bf16[256,768]{1,0:T(8,128)(2,1)S(1)}, bf16[256,768]{1,0:T(8,128)(2,1)S(1)}, u32[]{:S(2)}, u32[]{:S(2)}) %collective-permute-start.7) | collective-permute-done | bytes 393248 | tf_op jit(solution)/shard_map/ppermute | solution.py:59
  78.8 2.4 %add_convert_fusion.1 = bf16[256,768]{1,0:T(8,128)(2,1)S(1)} fusion(bf16[256,768]{1,0:T(8,128)(2,1)S(1)} %collective-permute-done.7, bf16[2,256,768]{2,1,0:T(8,128)(2,1)S(1)} %bitcast.40, bf16[2,768,3072]{2,1,0:T(8,128)(2,1)} %param.10, s32[]{:T(128)S(6)} %select_n.129), kind=kOutput, calls=%fused_computation.17 | convolution fusion | flops 604569600 | bytes 3932164 | tf_op jit(solution)/shard_map/qtb,qbc->tc/dot_general | solution.py:57
  81.3 2.4 %fusion.20 = bf16[256,768]{1,0:T(8,128)(2,1)S(1)} fusion(bf16[2,256,768]{2,1,0:T(8,128)(2,1)S(1)} %bitcast.41, bf16[2,768,3072]{2,1,0:T(8,128)(2,1)} %param.10, s32[]{:T(128)S(6)} %select_n.132), kind=kOutput, calls=%fused_computation.13 | convolution fusion | flops 604176384 | bytes 3538948 | tf_op jit(solution)/shard_map/qtb,qbc->tc/dot_general | solution.py:57
  83.7 2.3 %collective-permute-start.8 = (bf16[256,768]{1,0:T(8,128)(2,1)S(1)}, bf16[256,768]{1,0:T(8,128)(2,1)S(1)}, u32[]{:S(2)}, u32[]{:S(2)}) collective-permute-start(bf16[256,768]{1,0:T(8,128)(2,1)S(1)} %fusion.20), channel_id=1, source_target_pairs={{0,1},{1,0},{2,3},{3,2},{4,5},{5,4},{6,7},{7,6},{8,9},{9,8},{10,11... | collective-permute-start | bytes 1179656 | tf_op jit(solution)/shard_map/ppermute | solution.py:63
  86.0 4.4 %collective-permute-start.9 = (bf16[256,768]{1,0:T(8,128)(2,1)S(1)}, bf16[256,768]{1,0:T(8,128)(2,1)S(1)}, u32[]{:S(2)}, u32[]{:S(2)}) collective-permute-start(bf16[256,768]{1,0:T(8,128)(2,1)S(1)} %add_convert_fusion.1), channel_id=1, source_target_pairs={{0,2},{2,0},{1,3},{3,1},{4,6},{6,4},{5,7},{7,5},{8,10},{10,8},{9,1... | collective-permute-start | bytes 1179656 | tf_op jit(solution)/shard_map/ppermute | solution.py:62
  90.4 0.0 copy-start
  90.4 2.5 %fusion.14 = f32[256,768]{1,0:T(8,128)S(1)} fusion(bf16[2,256,768]{2,1,0:T(8,128)(2,1)S(1)} %bitcast.42, bf16[2,768,3072]{2,1,0:T(8,128)(2,1)} %param.10, s32[]{:T(128)S(6)} %select_n.131), kind=kOutput, calls=%fused_computation.11 | convolution fusion | flops 603979776 | bytes 3932164 | tf_op jit(solution)/shard_map/qtb,qbc->tc/dot_general | solution.py:57
  92.9 0.0 collective-permute-done.8
  92.9 7.1 %collective-permute-done.9 = bf16[256,768]{1,0:T(8,128)(2,1)S(1)} collective-permute-done((bf16[256,768]{1,0:T(8,128)(2,1)S(1)}, bf16[256,768]{1,0:T(8,128)(2,1)S(1)}, u32[]{:S(2)}, u32[]{:S(2)}) %collective-permute-start.9) | collective-permute-done | bytes 393248 | tf_op jit(solution)/shard_map/ppermute | solution.py:62
  100.0 0.0 copy-done
  100.0 1.4 %negate_divide_fusion = (f32[256,768]{1,0:T(8,128)}, f32[256,768]{1,0:T(8,128)}) fusion(f32[256,768]{1,0:T(8,128)S(1)} %copy-done, bf16[256,768]{1,0:T(8,128)(2,1)S(1)} %collective-permute-done.9, f32[256,768]{1,0:T(8,128)S(1)} %fusion.14, bf16[256,768]{1,0:T(8,128)(2,1)S(1)} %collective-permute-done.8), kind=kLoop, calls=%fused_computation.15 | loop fusion | flops 1376256 | bytes 3932160 | tf_op jit(solution)/shard_map/div | solution.py:65
  (1 shorter events, 0.0 us)
Async XLA Ops:
  2.1 39.4 %all-to-all-start = ((bf16[24,8,768]{2,1,0:T(8,128)(2,1)}), bf16[24,8,768]{2,1,0:T(8,128)(2,1)S(1)}, u32[]{:S(2)}, u32[]{:S(2)}) async-start(bf16[24,8,768]{2,1,0:T(8,128)(2,1)} %broadcast_in_dim.7), calls=%async_computation | async-start | bytes 589824 | tf_op jit(solution)/shard_map/all_to_all | solution.py:33
  41.4 14.3 %collective-permute-start.3 = (bf16[192,768]{1,0:T(8,128)(2,1)S(1)}, bf16[192,768]{1,0:T(8,128)(2,1)S(1)}, u32[]{:S(2)}, u32[]{:S(2)}) collective-permute-start(bf16[192,768]{1,0:T(8,128)(2,1)S(1)} %bitcast.43), channel_id=1, source_target_pairs={{0,384},{1,385},{2,386},{3,387},{4,388},{5,389},{6,390},{7,391},{8... | collective-permute-start | bytes 884744 | tf_op jit(solution)/shard_map/ppermute | solution.py:34
  44.6 15.9 %collective-permute-start = (bf16[192,768]{1,0:T(8,128)(2,1)S(1)}, bf16[192,768]{1,0:T(8,128)(2,1)S(1)}, u32[]{:S(2)}, u32[]{:S(2)}) collective-permute-start(bf16[192,768]{1,0:T(8,128)(2,1)S(1)} %bitcast.44), channel_id=1, source_target_pairs={{0,36},{1,381},{2,38},{3,383},{4,40},{5,353},{6,42},{7,355},{8,44}... | collective-permute-start | bytes 884744 | tf_op jit(solution)/shard_map/ppermute | solution.py:36
  50.5 12.4 %collective-permute-start.1 = (bf16[192,768]{1,0:T(8,128)(2,1)S(1)}, bf16[192,768]{1,0:T(8,128)(2,1)S(1)}, u32[]{:S(2)}, u32[]{:S(2)}) collective-permute-start(bf16[192,768]{1,0:T(8,128)(2,1)S(1)} %bitcast.45), channel_id=1, source_target_pairs={{0,32},{1,353},{2,34},{3,355},{4,36},{5,357},{6,38},{7,359},{8,40}... | collective-permute-start | bytes 884744 | tf_op jit(solution)/shard_map/ppermute | solution.py:36
  52.4 10.8 %collective-permute-start.2 = (bf16[192,768]{1,0:T(8,128)(2,1)S(1)}, bf16[192,768]{1,0:T(8,128)(2,1)S(1)}, u32[]{:S(2)}, u32[]{:S(2)}) collective-permute-start(bf16[192,768]{1,0:T(8,128)(2,1)S(1)} %bitcast.46), channel_id=1, source_target_pairs={{0,4},{1,29},{2,6},{3,31},{4,8},{5,1},{6,10},{7,3},{8,12},{9,5},{1... | collective-permute-start | bytes 884744 | tf_op jit(solution)/shard_map/ppermute | solution.py:36
  55.8 8.4 %collective-permute-start.4 = (bf16[192,768]{1,0:T(8,128)(2,1)S(1)}, bf16[192,768]{1,0:T(8,128)(2,1)S(1)}, u32[]{:S(2)}, u32[]{:S(2)}) collective-permute-start(bf16[192,768]{1,0:T(8,128)(2,1)S(1)} %collective-permute-done.3), channel_id=1, source_target_pairs={{0,36},{1,381},{2,38},{3,383},{4,40},{5,353},{6,42},{7,355},{8,44}... | collective-permute-start | bytes 884744 | tf_op jit(solution)/shard_map/ppermute | solution.py:38
  58.0 8.7 %collective-permute-start.5 = (bf16[192,768]{1,0:T(8,128)(2,1)S(1)}, bf16[192,768]{1,0:T(8,128)(2,1)S(1)}, u32[]{:S(2)}, u32[]{:S(2)}) collective-permute-start(bf16[192,768]{1,0:T(8,128)(2,1)S(1)} %collective-permute-done.3), channel_id=1, source_target_pairs={{0,32},{1,353},{2,34},{3,355},{4,36},{5,357},{6,38},{7,359},{8,40}... | collective-permute-start | bytes 884744 | tf_op jit(solution)/shard_map/ppermute | solution.py:38
  60.5 7.8 %collective-permute-start.6 = (bf16[192,768]{1,0:T(8,128)(2,1)S(1)}, bf16[192,768]{1,0:T(8,128)(2,1)S(1)}, u32[]{:S(2)}, u32[]{:S(2)}) collective-permute-start(bf16[192,768]{1,0:T(8,128)(2,1)S(1)} %collective-permute-done.3), channel_id=1, source_target_pairs={{0,4},{1,29},{2,6},{3,31},{4,8},{5,1},{6,10},{7,3},{8,12},{9,5},{1... | collective-permute-start | bytes 884744 | tf_op jit(solution)/shard_map/ppermute | solution.py:38
  71.5 7.4 %collective-permute-start.7 = (bf16[256,768]{1,0:T(8,128)(2,1)S(1)}, bf16[256,768]{1,0:T(8,128)(2,1)S(1)}, u32[]{:S(2)}, u32[]{:S(2)}) collective-permute-start(bf16[256,768]{1,0:T(8,128)(2,1)S(1)} %fusion.23), channel_id=1, source_target_pairs={{0,1},{1,0},{2,3},{3,2},{4,5},{5,4},{6,7},{7,6},{8,9},{9,8},{10,11... | collective-permute-start | bytes 1179656 | tf_op jit(solution)/shard_map/ppermute | solution.py:59
  83.7 9.2 %collective-permute-start.8 = (bf16[256,768]{1,0:T(8,128)(2,1)S(1)}, bf16[256,768]{1,0:T(8,128)(2,1)S(1)}, u32[]{:S(2)}, u32[]{:S(2)}) collective-permute-start(bf16[256,768]{1,0:T(8,128)(2,1)S(1)} %fusion.20), channel_id=1, source_target_pairs={{0,1},{1,0},{2,3},{3,2},{4,5},{5,4},{6,7},{7,6},{8,9},{9,8},{10,11... | collective-permute-start | bytes 1179656 | tf_op jit(solution)/shard_map/ppermute | solution.py:63
  86.0 14.0 %collective-permute-start.9 = (bf16[256,768]{1,0:T(8,128)(2,1)S(1)}, bf16[256,768]{1,0:T(8,128)(2,1)S(1)}, u32[]{:S(2)}, u32[]{:S(2)}) collective-permute-start(bf16[256,768]{1,0:T(8,128)(2,1)S(1)} %add_convert_fusion.1), channel_id=1, source_target_pairs={{0,2},{2,0},{1,3},{3,1},{4,6},{6,4},{5,7},{7,5},{8,10},{10,8},{9,1... | collective-permute-start | bytes 1179656 | tf_op jit(solution)/shard_map/ppermute | solution.py:62
  90.4 9.6 %copy-start = (f32[256,768]{1,0:T(8,128)S(1)}, f32[256,768]{1,0:T(8,128)}, u32[]{:S(2)}) copy-start(f32[256,768]{1,0:T(8,128)} %param.11) | copy-start | bytes 2359300

commit v3 on v2

--- a/solution.py
+++ b/solution.py
@@ -1,6 +1,8 @@
 import jax
 import jax.numpy as jnp
 from jax import lax
+from jax.experimental import pallas as pl
+from jax.experimental.pallas import tpu as pltpu
 from jax.sharding import Mesh
 from jax.sharding import PartitionSpec as P
 
@@ -10,6 +12,7 @@
 FAR = ("zh", "yh")
 NEAR = ((1, 1), (1, 0), (0, 1))
 SWAP = [(0, 1), (1, 0)]
+STEP = 256
 
 
 def shift(dx, dz, dy):
@@ -18,10 +21,64 @@
         for z in range(12):
             for y in range(8):
                 for k in range(4):
-                    s = -1 if k % 2 else 1
+                    s = 1 if k % 2 else -1
                     there = (((x + dx) % 2) * 12 + (z + s * dz) % 12) * 8 + (y + s * dy) % 8
                     pairs.append((((x * 12 + z) * 8 + y) * 4 + k, there * 4 + k))
     return pairs
+
+
+def contract_kernel(starts, rows_ref, table_ref, out_ref, held, sems):
+    parts, depth, width = out_ref.shape[0], rows_ref.shape[1], out_ref.shape[2]
+    tile_rows = out_ref.shape[1]
+    blocks = [(q, k) for q in range(table_ref.shape[0]) for k in range(depth // STEP)]
+    copies = []
+    for p in range(parts):
+        start = pl.multiple_of(starts[p], 128)
+        for at, (q, k) in enumerate(blocks):
+            copy = pltpu.make_async_copy(
+                table_ref.at[q, pl.ds(k * STEP, STEP), pl.ds(start, width)],
+                held.at[p, at],
+                sems.at[p, at],
+            )
+            copy.start()
+            copies.append(copy)
+    for p in range(parts):
+        total = None
+        for at, (q, k) in enumerate(blocks):
+            copies[p * len(blocks) + at].wait()
+            term = jnp.dot(
+                rows_ref[q * tile_rows:(q + 1) * tile_rows, k * STEP:(k + 1) * STEP],
+                held[p, at],
+                preferred_element_type=jnp.float32,
+            )
+            total = term if total is None else total + term
+        out_ref[p] = total.astype(out_ref.dtype)
+
+
+def contract(rows, table, starts, kinds):
+    blocks, depth, columns = table.shape
+    parts, tile_rows, width = starts.shape[0], rows.shape[0] // blocks, rows.shape[1]
+    count = blocks * (depth // STEP)
+    return pl.pallas_call(
+        contract_kernel,
+        out_shape=[jax.ShapeDtypeStruct((parts, tile_rows, width), kind) for kind in kinds],
+        in_specs=[
+            pl.BlockSpec(memory_space=pltpu.SMEM),
+            pl.BlockSpec(memory_space=pltpu.VMEM),
+            pl.BlockSpec(memory_space=pl.ANY),
+        ],
+        out_specs=[pl.BlockSpec(memory_space=pltpu.VMEM) for _ in kinds],
+        scratch_shapes=[
+            pltpu.VMEM((parts, count, STEP, width), table.dtype),
+            pltpu.SemaphoreType.DMA((parts, count)),
+        ],
+        compiler_params=pltpu.CompilerParams(vmem_limit_bytes=24 << 20),
+        cost_estimate=pl.CostEstimate(
+            flops=2 * parts * tile_rows * blocks * depth * width,
+            bytes_accessed=2 * parts * blocks * depth * width,
+            transcendentals=0,
+        ),
+    )(starts, rows, table)
 
 
 def shards(core_coef, dest_rows, block_ids, bin_offsets, couplings, energy_gap):
@@ -50,18 +107,18 @@
         row = target[(xl + dx) % 2, (zl + dz) % 2, (yl + dy) % 2]
         onehot = (slots[:, None] == row[None, :]).astype(jnp.bfloat16)
         summed = summed + jnp.dot(onehot, piece, preferred_element_type=jnp.float32)
-    gathered = summed.astype(jnp.bfloat16).reshape(2, tile_rows, width)
+    gathered = summed.astype(jnp.bfloat16)
 
-    def columns(rows, h, k):
-        block = lax.dynamic_slice_in_dim(couplings, (h * 2 + k) * width, width, 2)
-        return jnp.einsum("qtb,qbc->tc", rows, block, preferred_element_type=jnp.float32)
-
-    far_in = lax.ppermute(columns(gathered, 1 - xh, 1 - c).astype(jnp.bfloat16), "c", SWAP)
-    far = (columns(gathered, 1 - xh, c) + far_in.astype(jnp.float32)).astype(jnp.bfloat16)
-    far, gathered = lax.optimization_barrier((far, gathered))
-    far = lax.ppermute(far, "xh", SWAP)
-    near_in = lax.ppermute(columns(gathered, xh, 1 - c).astype(jnp.bfloat16), "c", SWAP)
-    numerators = columns(gathered, xh, c) + near_in.astype(jnp.float32) + far.astype(jnp.float32)
+    far_out, near_out = (xh * -2 + 2 + 1 - c), (xh * 2 + 1 - c)
+    far_own, near_own = (xh * -2 + 2 + c), (xh * 2 + c)
+    out = contract(gathered, couplings, jnp.stack([far_out, near_out]) * width, (jnp.bfloat16,))
+    beside_in = lax.ppermute(out[0], "c", SWAP)
+    sums = contract(
+        gathered, couplings, jnp.stack([far_own, near_own]) * width, (jnp.float32,)
+    )[0]
+    far = (sums[0] + beside_in[0].astype(jnp.float32)).astype(jnp.bfloat16)
+    far_in = lax.ppermute(far, "xh", SWAP)
+    numerators = sums[1] + beside_in[1].astype(jnp.float32) + far_in.astype(jnp.float32)
     energies = -(numerators * numerators) / energy_gap
     return (numerators, energies)
 

time: 102 us -> 103 us (level)
  matrix products: 13.1 us -> 3.21 us
  Pallas kernels: 0 us -> 8.32 us
  local copies, waits for them, and re-layouts: 2.75 us -> 7.01 us
  starting transfers between devices: 53.4 us -> 49.3 us
  waiting for transfers between devices: 27.5 us -> 29.5 us
    dot_general x4 -> x0, matrix products: 9.84 us -> none  [columns(): jnp.einsum('qtb,qbc->tc', rows, block, preferred_element_type=jnp.float32)]
    pallas_call x0 -> x2, Pallas kernels: none -> 8.32 us  [contract(): pl.pallas_call(contract_kernel, out_shape=[jax.ShapeDtypeStruct((parts, t...]
    unnamed x3 -> x11, local copies, waits for them, and re-layouts: 0.52 us -> 4.77 us
    ppermute x3 -> x2, starting transfers between devices: 12.7 us -> 9.47 us  [the longest x1 4.98 us: shards(): beside_in = lax.ppermute(out[0], 'c', SWAP)]
    ppermute x3, starting transfers between devices: 10.7 us -> 8.98 us  [shards(): lax.ppermute(own, NAMES, shift(0, *at))]
    ppermute x3 -> x2, waiting for transfers between devices: 8.39 us -> 9.77 us  [the longest x1 9.76 us: shards(): far_in = lax.ppermute(far, 'xh', SWAP)]
  transfers between devices with their start and end apart: 11 -> 10, of which waited for: 6 -> 5; matrix products, arithmetic and copies ran while one was open for 8% -> 6% of each run, Pallas kernels for 0% -> 4%
where the time goes in v3:
time: 103 us; the launch traced here: 102 us
  starting transfers between devices  49.3 us (48%)
  waiting for transfers between devices  29.5 us (29%)
  Pallas kernels  8.32 us (8%)
  local copies, waits for them, and re-layouts  7.01 us (7%)
  other arithmetic  3.83 us (4%)
  matrix products  3.21 us (3%)
    all_to_all x1, starting transfers between devices, shards(): own = lax.all_to_all(spread, FAR, 0, 0, tiled=True).reshape(192, width)  20.6 us
    all_to_all x1, waiting for transfers between devices, shards(): own = lax.all_to_all(spread, FAR, 0, 0, tiled=True).reshape(192, width)  15.1 us
    ppermute x1, waiting for transfers between devices, shards(): far_in = lax.ppermute(far, 'xh', SWAP)  9.76 us
    ppermute x3, starting transfers between devices, shards(): lax.ppermute(own, NAMES, shift(0, *at))  8.98 us
    pallas_call x2, Pallas kernels, contract(): pl.pallas_call(contract_kernel, out_shape=[jax.ShapeDtypeStruct((parts, t...  8.32 us
    ppermute x3, starting transfers between devices, shards(): lax.ppermute(beside, NAMES, shift(0, *at))  7.15 us
    ppermute x1, starting transfers between devices, shards(): beside_in = lax.ppermute(out[0], 'c', SWAP)  4.98 us
    unnamed x11, local copies, waits for them, and re-layouts  4.77 us
  transfers between devices with their start and end apart: 10, of which 5 were waited for; matrix products, arithmetic and copies ran while one was open for 6% of the time, Pallas kernels for 4%

profile of v3, /device:TPU:1, one launch (start us, length us, event | category | flops | bytes accessed | tf_op | source)
XLA Modules:
  0.0 102.2 jit_solution(5741315872193378339)
XLA Ops:
  0.6 1.4 %broadcast_in_dim.7 = bf16[24,8,768]{2,1,0:T(8,128)(2,1)} broadcast(bf16[8,768]{1,0:T(8,128)(2,1)} %param.6), dimensions={1,2} | broadcast | bytes 307200 | tf_op jit(solution)/shard_map/broadcast_in_dim | solution.py:89
  2.1 20.6 %all-to-all-start = ((bf16[24,8,768]{2,1,0:T(8,128)(2,1)}), bf16[24,8,768]{2,1,0:T(8,128)(2,1)S(1)}, u32[]{:S(2)}, u32[]{:S(2)}) async-start(bf16[24,8,768]{2,1,0:T(8,128)(2,1)} %broadcast_in_dim.7), calls=%async_computation | async-start | bytes 589824 | tf_op jit(solution)/shard_map/all_to_all | solution.py:90
  22.7 0.7 add_reduce_fusion
  23.4 0.2 add.154
  23.6 0.5 broadcast.26
  24.2 1.3 %reduce.5 = s32[192]{0:T(256)S(1)} reduce(s32[1,192]{1,0:T(1,128)} %param.9, s32[]{:T(128)} %broadcast.26), dimensions={0}, to_apply=%param.9.reduce_sub_computation.3 | reduce | bytes 1540 | tf_op args[3]
  25.5 0.2 lt.115
  25.7 0.3 copy.8
  26.0 0.1 fusion.20
  26.1 0.1 reshape.39
  26.3 15.1 %all-to-all-done = bf16[24,8,768]{2,1,0:T(8,128)(2,1)S(1)} async-done(((bf16[24,8,768]{2,1,0:T(8,128)(2,1)}), bf16[24,8,768]{2,1,0:T(8,128)(2,1)S(1)}, u32[]{:S(2)}, u32[]{:S(2)}) %all-to-all-start) | async-done | bytes 294944 | tf_op jit(solution)/shard_map/all_to_all | solution.py:90
  41.4 3.1 %collective-permute-start.3 = (bf16[192,768]{1,0:T(8,128)(2,1)S(1)}, bf16[192,768]{1,0:T(8,128)(2,1)S(1)}, u32[]{:S(2)}, u32[]{:S(2)}) collective-permute-start(bf16[192,768]{1,0:T(8,128)(2,1)S(1)} %bitcast.33), channel_id=1, source_target_pairs={{0,384},{1,385},{2,386},{3,387},{4,388},{5,389},{6,390},{7,391},{8... | collective-permute-start | bytes 884744 | tf_op jit(solution)/shard_map/ppermute | solution.py:91
  44.6 0.1 add_multiply_fusion.1.starts
  44.6 4.9 %collective-permute-start = (bf16[192,768]{1,0:T(8,128)(2,1)S(1)}, bf16[192,768]{1,0:T(8,128)(2,1)S(1)}, u32[]{:S(2)}, u32[]{:S(2)}) collective-permute-start(bf16[192,768]{1,0:T(8,128)(2,1)S(1)} %bitcast.34), channel_id=1, source_target_pairs={{0,380},{1,37},{2,382},{3,39},{4,352},{5,41},{6,354},{7,43},{8,356... | collective-permute-start | bytes 884744 | tf_op jit(solution)/shard_map/ppermute | solution.py:93
  49.5 1.9 %collective-permute-start.1 = (bf16[192,768]{1,0:T(8,128)(2,1)S(1)}, bf16[192,768]{1,0:T(8,128)(2,1)S(1)}, u32[]{:S(2)}, u32[]{:S(2)}) collective-permute-start(bf16[192,768]{1,0:T(8,128)(2,1)S(1)} %bitcast.35), channel_id=1, source_target_pairs={{0,352},{1,33},{2,354},{3,35},{4,356},{5,37},{6,358},{7,39},{8,360... | collective-permute-start | bytes 884744 | tf_op jit(solution)/shard_map/ppermute | solution.py:93
  51.4 2.2 %collective-permute-start.2 = (bf16[192,768]{1,0:T(8,128)(2,1)S(1)}, bf16[192,768]{1,0:T(8,128)(2,1)S(1)}, u32[]{:S(2)}, u32[]{:S(2)}) collective-permute-start(bf16[192,768]{1,0:T(8,128)(2,1)S(1)} %bitcast.36), channel_id=1, source_target_pairs={{0,28},{1,5},{2,30},{3,7},{4,0},{5,9},{6,2},{7,11},{8,4},{9,13},{1... | collective-permute-start | bytes 884744 | tf_op jit(solution)/shard_map/ppermute | solution.py:93
  53.6 0.4 fusion.3
  54.0 0.0 collective-permute-done.3
  54.0 3.0 %collective-permute-start.4 = (bf16[192,768]{1,0:T(8,128)(2,1)S(1)}, bf16[192,768]{1,0:T(8,128)(2,1)S(1)}, u32[]{:S(2)}, u32[]{:S(2)}) collective-permute-start(bf16[192,768]{1,0:T(8,128)(2,1)S(1)} %collective-permute-done.3), channel_id=1, source_target_pairs={{0,380},{1,37},{2,382},{3,39},{4,352},{5,41},{6,354},{7,43},{8,356... | collective-permute-start | bytes 884744 | tf_op jit(solution)/shard_map/ppermute | solution.py:95
  57.1 1.9 %collective-permute-start.5 = (bf16[192,768]{1,0:T(8,128)(2,1)S(1)}, bf16[192,768]{1,0:T(8,128)(2,1)S(1)}, u32[]{:S(2)}, u32[]{:S(2)}) collective-permute-start(bf16[192,768]{1,0:T(8,128)(2,1)S(1)} %collective-permute-done.3), channel_id=1, source_target_pairs={{0,352},{1,33},{2,354},{3,35},{4,356},{5,37},{6,358},{7,39},{8,360... | collective-permute-start | bytes 884744 | tf_op jit(solution)/shard_map/ppermute | solution.py:95
  59.0 0.4 fusion.7
  59.4 0.0 collective-permute-done
  59.4 2.2 %collective-permute-start.6 = (bf16[192,768]{1,0:T(8,128)(2,1)S(1)}, bf16[192,768]{1,0:T(8,128)(2,1)S(1)}, u32[]{:S(2)}, u32[]{:S(2)}) collective-permute-start(bf16[192,768]{1,0:T(8,128)(2,1)S(1)} %collective-permute-done.3), channel_id=1, source_target_pairs={{0,28},{1,5},{2,30},{3,7},{4,0},{5,9},{6,2},{7,11},{8,4},{9,13},{1... | collective-permute-start | bytes 884744 | tf_op jit(solution)/shard_map/ppermute | solution.py:95
  61.6 0.0 slice-start
  61.6 0.4 fusion.4
  62.0 0.0 collective-permute-done.1
  62.0 0.4 fusion.5
  62.4 0.0 collective-permute-done.2
  62.4 0.4 fusion.6
  62.8 2.1 %collective-permute-done.4 = bf16[192,768]{1,0:T(8,128)(2,1)S(1)} collective-permute-done((bf16[192,768]{1,0:T(8,128)(2,1)S(1)}, bf16[192,768]{1,0:T(8,128)(2,1)S(1)}, u32[]{:S(2)}, u32[]{:S(2)}) %collective-permute-start.4) | collective-permute-done | bytes 294944 | tf_op jit(solution)/shard_map/ppermute | solution.py:95
  64.8 0.0 slice-start.1
  64.8 0.4 fusion.8
  65.2 0.7 collective-permute-done.5
  65.9 0.4 fusion.9
  66.3 1.8 %collective-permute-done.6 = bf16[192,768]{1,0:T(8,128)(2,1)S(1)} collective-permute-done((bf16[192,768]{1,0:T(8,128)(2,1)S(1)}, bf16[192,768]{1,0:T(8,128)(2,1)S(1)}, u32[]{:S(2)}, u32[]{:S(2)}) %collective-permute-start.6) | collective-permute-done | bytes 294944 | tf_op jit(solution)/shard_map/ppermute | solution.py:95
  68.1 0.0 slice-start.2
  68.1 0.6 add_convert_fusion.rows_ref
  68.7 0.0 slice-done
  68.7 0.0 slice-done.1
  68.7 0.6 slice-done.2
  69.3 4.2 %shard_map.78 = bf16[2,256,768]{2,1,0:T(8,128)(2,1)S(1)} custom-call(s32[2]{0:T(128)S(1)} %add_multiply_fusion.1.starts, bf16[512,768]{1,0:T(8,128)(2,1)S(1)} %add_convert_fusion.rows_ref, bf16[2,768,3072]{2,1,0:T(8,128)(2,1)S(1)} %bitcast.32), custom_call_target="tpu_custom_call" | custom-call | flops 1207959552 | bytes 4718592 | tf_op jit(solution)/shard_map/pallas_call | solution.py:62
  73.5 5.0 %collective-permute-start.7 = (bf16[2,256,768]{2,1,0:T(8,128)(2,1)S(1)}, bf16[2,256,768]{2,1,0:T(8,128)(2,1)S(1)}, u32[]{:S(2)}, u32[]{:S(2)}) collective-permute-start(bf16[2,256,768]{2,1,0:T(8,128)(2,1)S(1)} %shard_map.78), channel_id=1, source_target_pairs={{0,1},{1,0},{2,3},{3,2},{4,5},{5,4},{6,7},{7,6},{8,9},{9,8},{10,11... | collective-permute-start | bytes 2359304 | tf_op jit(solution)/shard_map/ppermute | solution.py:115
  78.5 0.1 add_multiply_fusion.starts
  78.5 0.0 copy-start
  78.5 3.7 %copy-done = bf16[2,768,3072]{2,1,0:T(8,128)(2,1)S(1)} copy-done((bf16[2,768,3072]{2,1,0:T(8,128)(2,1)S(1)}, bf16[2,768,3072]{2,1,0:T(8,128)(2,1)}, u32[]{:S(2)}) %copy-start) | copy-done | bytes 9437208
  82.2 4.2 %shard_map.77 = f32[2,256,768]{2,1,0:T(8,128)S(1)} custom-call(s32[2]{0:T(128)S(1)} %add_multiply_fusion.starts, bf16[512,768]{1,0:T(8,128)(2,1)S(1)} %add_convert_fusion.rows_ref, bf16[2,768,3072]{2,1,0:T(8,128)(2,1)S(1)} %copy-done), custom_call_target="tpu_custom_call" | custom-call | flops 1207959552 | bytes 4718592 | tf_op jit(solution)/shard_map/pallas_call | solution.py:62
  86.4 0.0 copy-start.1
  86.4 0.0 collective-permute-done.7
  86.4 0.1 fusion.11
  86.5 4.5 %collective-permute-start.8 = (bf16[256,768]{1,0:T(8,128)(2,1)S(1)}, bf16[256,768]{1,0:T(8,128)(2,1)S(1)}, u32[]{:S(2)}, u32[]{:S(2)}) collective-permute-start(bf16[256,768]{1,0:T(8,128)(2,1)S(1)} %fusion.11), channel_id=1, source_target_pairs={{0,2},{2,0},{1,3},{3,1},{4,6},{6,4},{5,7},{7,5},{8,10},{10,8},{9,1... | collective-permute-start | bytes 1179656 | tf_op jit(solution)/shard_map/ppermute | solution.py:120
  91.0 9.8 %collective-permute-done.8 = bf16[256,768]{1,0:T(8,128)(2,1)S(1)} collective-permute-done((bf16[256,768]{1,0:T(8,128)(2,1)S(1)}, bf16[256,768]{1,0:T(8,128)(2,1)S(1)}, u32[]{:S(2)}, u32[]{:S(2)}) %collective-permute-start.8) | collective-permute-done | bytes 393248 | tf_op jit(solution)/shard_map/ppermute | solution.py:120
  100.8 0.0 copy-done.1
  100.8 1.4 %negate_divide_fusion = (f32[256,768]{1,0:T(8,128)}, f32[256,768]{1,0:T(8,128)}) fusion(f32[256,768]{1,0:T(8,128)S(1)} %copy-done.1, bf16[256,768]{1,0:T(8,128)(2,1)S(1)} %collective-permute-done.8, bf16[2,256,768]{2,1,0:T(8,128)(2,1)S(1)} %collective-permute-done.7, f32[2,256,768]{2,1,0:T(8,128)S(1)} %shard_map.77), kind=kLoop, calls=%fused_computation.6 | loop fusion | flops 1376256 | bytes 3932160 | tf_op jit(solution)/shard_map/div | solution.py:122
  (2 shorter events, 0.0 us)
Async XLA Ops:
  2.1 39.4 %all-to-all-start = ((bf16[24,8,768]{2,1,0:T(8,128)(2,1)}), bf16[24,8,768]{2,1,0:T(8,128)(2,1)S(1)}, u32[]{:S(2)}, u32[]{:S(2)}) async-start(bf16[24,8,768]{2,1,0:T(8,128)(2,1)} %broadcast_in_dim.7), calls=%async_computation | async-start | bytes 589824 | tf_op jit(solution)/shard_map/all_to_all | solution.py:90
  41.4 12.6 %collective-permute-start.3 = (bf16[192,768]{1,0:T(8,128)(2,1)S(1)}, bf16[192,768]{1,0:T(8,128)(2,1)S(1)}, u32[]{:S(2)}, u32[]{:S(2)}) collective-permute-start(bf16[192,768]{1,0:T(8,128)(2,1)S(1)} %bitcast.33), channel_id=1, source_target_pairs={{0,384},{1,385},{2,386},{3,387},{4,388},{5,389},{6,390},{7,391},{8... | collective-permute-start | bytes 884744 | tf_op jit(solution)/shard_map/ppermute | solution.py:91
  44.6 14.7 %collective-permute-start = (bf16[192,768]{1,0:T(8,128)(2,1)S(1)}, bf16[192,768]{1,0:T(8,128)(2,1)S(1)}, u32[]{:S(2)}, u32[]{:S(2)}) collective-permute-start(bf16[192,768]{1,0:T(8,128)(2,1)S(1)} %bitcast.34), channel_id=1, source_target_pairs={{0,380},{1,37},{2,382},{3,39},{4,352},{5,41},{6,354},{7,43},{8,356... | collective-permute-start | bytes 884744 | tf_op jit(solution)/shard_map/ppermute | solution.py:93
  49.5 12.5 %collective-permute-start.1 = (bf16[192,768]{1,0:T(8,128)(2,1)S(1)}, bf16[192,768]{1,0:T(8,128)(2,1)S(1)}, u32[]{:S(2)}, u32[]{:S(2)}) collective-permute-start(bf16[192,768]{1,0:T(8,128)(2,1)S(1)} %bitcast.35), channel_id=1, source_target_pairs={{0,352},{1,33},{2,354},{3,35},{4,356},{5,37},{6,358},{7,39},{8,360... | collective-permute-start | bytes 884744 | tf_op jit(solution)/shard_map/ppermute | solution.py:93
  51.4 10.9 %collective-permute-start.2 = (bf16[192,768]{1,0:T(8,128)(2,1)S(1)}, bf16[192,768]{1,0:T(8,128)(2,1)S(1)}, u32[]{:S(2)}, u32[]{:S(2)}) collective-permute-start(bf16[192,768]{1,0:T(8,128)(2,1)S(1)} %bitcast.36), channel_id=1, source_target_pairs={{0,28},{1,5},{2,30},{3,7},{4,0},{5,9},{6,2},{7,11},{8,4},{9,13},{1... | collective-permute-start | bytes 884744 | tf_op jit(solution)/shard_map/ppermute | solution.py:93
  54.0 10.8 %collective-permute-start.4 = (bf16[192,768]{1,0:T(8,128)(2,1)S(1)}, bf16[192,768]{1,0:T(8,128)(2,1)S(1)}, u32[]{:S(2)}, u32[]{:S(2)}) collective-permute-start(bf16[192,768]{1,0:T(8,128)(2,1)S(1)} %collective-permute-done.3), channel_id=1, source_target_pairs={{0,380},{1,37},{2,382},{3,39},{4,352},{5,41},{6,354},{7,43},{8,356... | collective-permute-start | bytes 884744 | tf_op jit(solution)/shard_map/ppermute | solution.py:95
  57.1 8.8 %collective-permute-start.5 = (bf16[192,768]{1,0:T(8,128)(2,1)S(1)}, bf16[192,768]{1,0:T(8,128)(2,1)S(1)}, u32[]{:S(2)}, u32[]{:S(2)}) collective-permute-start(bf16[192,768]{1,0:T(8,128)(2,1)S(1)} %collective-permute-done.3), channel_id=1, source_target_pairs={{0,352},{1,33},{2,354},{3,35},{4,356},{5,37},{6,358},{7,39},{8,360... | collective-permute-start | bytes 884744 | tf_op jit(solution)/shard_map/ppermute | solution.py:95
  59.4 8.7 %collective-permute-start.6 = (bf16[192,768]{1,0:T(8,128)(2,1)S(1)}, bf16[192,768]{1,0:T(8,128)(2,1)S(1)}, u32[]{:S(2)}, u32[]{:S(2)}) collective-permute-start(bf16[192,768]{1,0:T(8,128)(2,1)S(1)} %collective-permute-done.3), channel_id=1, source_target_pairs={{0,28},{1,5},{2,30},{3,7},{4,0},{5,9},{6,2},{7,11},{8,4},{9,13},{1... | collective-permute-start | bytes 884744 | tf_op jit(solution)/shard_map/ppermute | solution.py:95
  61.6 7.1 %slice-start = ((s8[9437184]{0:T(1024)(128)(4,1)}), s8[4194304]{0:T(1024)(128)(4,1)S(1)}, s32[]{:S(2)}) async-start(s8[9437184]{0:T(1024)(128)(4,1)} %bitcast.31), calls=%async_computation.1 | async-start | bytes 8388608
  64.8 3.9 %slice-start.1 = ((s8[9437184]{0:T(1024)(128)(4,1)}), s8[4194304]{0:T(1024)(128)(4,1)S(1)}, s32[]{:S(2)}) async-start(s8[9437184]{0:T(1024)(128)(4,1)} %bitcast.31), calls=%async_computation.2 | async-start | bytes 8388608
  68.1 1.2 %slice-start.2 = ((s8[9437184]{0:T(1024)(128)(4,1)}), s8[1048576]{0:T(1024)(128)(4,1)S(1)}, s32[]{:S(2)}) async-start(s8[9437184]{0:T(1024)(128)(4,1)} %bitcast.31), calls=%async_computation.3 | async-start | bytes 2097152
  73.5 12.9 %collective-permute-start.7 = (bf16[2,256,768]{2,1,0:T(8,128)(2,1)S(1)}, bf16[2,256,768]{2,1,0:T(8,128)(2,1)S(1)}, u32[]{:S(2)}, u32[]{:S(2)}) collective-permute-start(bf16[2,256,768]{2,1,0:T(8,128)(2,1)S(1)} %shard_map.78), channel_id=1, source_target_pairs={{0,1},{1,0},{2,3},{3,2},{4,5},{5,4},{6,7},{7,6},{8,9},{9,8},{10,11... | collective-permute-start | bytes 2359304 | tf_op jit(solution)/shard_map/ppermute | solution.py:115
  78.5 3.7 %copy-start = (bf16[2,768,3072]{2,1,0:T(8,128)(2,1)S(1)}, bf16[2,768,3072]{2,1,0:T(8,128)(2,1)}, u32[]{:S(2)}) copy-start(bf16[2,768,3072]{2,1,0:T(8,128)(2,1)} %table_ref.3) | copy-start | bytes 28311556
  86.4 14.4 %copy-start.1 = (f32[256,768]{1,0:T(8,128)S(1)}, f32[256,768]{1,0:T(8,128)}, u32[]{:S(2)}) copy-start(f32[256,768]{1,0:T(8,128)} %param.11) | copy-start | bytes 2359300
  86.5 14.3 %collective-permute-start.8 = (bf16[256,768]{1,0:T(8,128)(2,1)S(1)}, bf16[256,768]{1,0:T(8,128)(2,1)S(1)}, u32[]{:S(2)}, u32[]{:S(2)}) collective-permute-start(bf16[256,768]{1,0:T(8,128)(2,1)S(1)} %fusion.11), channel_id=1, source_target_pairs={{0,2},{2,0},{1,3},{3,1},{4,6},{6,4},{5,7},{7,5},{8,10},{10,8},{9,1... | collective-permute-start | bytes 1179656 | tf_op jit(solution)/shard_map/ppermute | solution.py:120

commit v4 on v2

--- a/solution.py
+++ b/solution.py
@@ -1,6 +1,8 @@
 import jax
 import jax.numpy as jnp
 from jax import lax
+from jax.experimental import pallas as pl
+from jax.experimental.pallas import tpu as pltpu
 from jax.sharding import Mesh
 from jax.sharding import PartitionSpec as P
 
@@ -8,7 +10,7 @@
 SIZES = (2, 6, 2, 4, 2, 2, 2)
 EXT = NAMES[:5]
 FAR = ("zh", "yh")
-NEAR = ((1, 1), (1, 0), (0, 1))
+NEAR = ((0, 1), (1, 0), (1, 1))
 SWAP = [(0, 1), (1, 0)]
 
 
@@ -18,10 +20,42 @@
         for z in range(12):
             for y in range(8):
                 for k in range(4):
-                    s = -1 if k % 2 else 1
+                    s = 1 if k % 2 else -1
                     there = (((x + dx) % 2) * 12 + (z + s * dz) % 12) * 8 + (y + s * dy) % 8
                     pairs.append((((x * 12 + z) * 8 + y) * 4 + k, there * 4 + k))
     return pairs
+
+
+def contract_kernel(rows_ref, *refs):
+    tables, out_ref = refs[:-1], refs[-1]
+    tile_rows = out_ref.shape[1]
+    for p, table_ref in enumerate(tables):
+        total = None
+        for q in range(table_ref.shape[0]):
+            term = jnp.dot(
+                rows_ref[q * tile_rows:(q + 1) * tile_rows, :],
+                table_ref[q],
+                preferred_element_type=jnp.float32,
+            )
+            total = term if total is None else total + term
+        out_ref[p] = total.astype(out_ref.dtype)
+
+
+def contract(rows, tables, kind):
+    blocks, depth, width = tables[0].shape
+    parts, tile_rows = len(tables), rows.shape[0] // blocks
+    return pl.pallas_call(
+        contract_kernel,
+        out_shape=jax.ShapeDtypeStruct((parts, tile_rows, width), kind),
+        in_specs=[pl.BlockSpec(memory_space=pltpu.VMEM) for _ in range(1 + parts)],
+        out_specs=pl.BlockSpec(memory_space=pltpu.VMEM),
+        compiler_params=pltpu.CompilerParams(vmem_limit_bytes=20 << 20),
+        cost_estimate=pl.CostEstimate(
+            flops=2 * parts * tile_rows * blocks * depth * width,
+            bytes_accessed=2 * parts * blocks * depth * width,
+            transcendentals=0,
+        ),
+    )(rows, *tables)
 
 
 def shards(core_coef, dest_rows, block_ids, bin_offsets, couplings, energy_gap):
@@ -31,6 +65,12 @@
     tile_rows = energy_gap.shape[0]
     spread = jnp.broadcast_to(core_coef[None], (24, group_rows, width))
     own = lax.all_to_all(spread, FAR, 0, 0, tiled=True).reshape(192, width)
+    tables = [
+        lax.dynamic_slice_in_dim(couplings, (h * 2 + k) * width, width, 2)
+        for k in (1 - c, c)
+        for h in (1 - xh, xh)
+    ]
+    own, tables = lax.optimization_barrier((own, tables))
     beside = lax.ppermute(own, NAMES, shift(1, 0, 0))
     pieces = [((0, 0, 0), own)]
     pieces += [((0,) + at, lax.ppermute(own, NAMES, shift(0, *at))) for at in NEAR]
@@ -50,18 +90,14 @@
         row = target[(xl + dx) % 2, (zl + dz) % 2, (yl + dy) % 2]
         onehot = (slots[:, None] == row[None, :]).astype(jnp.bfloat16)
         summed = summed + jnp.dot(onehot, piece, preferred_element_type=jnp.float32)
-    gathered = summed.astype(jnp.bfloat16).reshape(2, tile_rows, width)
+    gathered = summed.astype(jnp.bfloat16)
 
-    def columns(rows, h, k):
-        block = lax.dynamic_slice_in_dim(couplings, (h * 2 + k) * width, width, 2)
-        return jnp.einsum("qtb,qbc->tc", rows, block, preferred_element_type=jnp.float32)
-
-    far_in = lax.ppermute(columns(gathered, 1 - xh, 1 - c).astype(jnp.bfloat16), "c", SWAP)
-    far = (columns(gathered, 1 - xh, c) + far_in.astype(jnp.float32)).astype(jnp.bfloat16)
-    far, gathered = lax.optimization_barrier((far, gathered))
-    far = lax.ppermute(far, "xh", SWAP)
-    near_in = lax.ppermute(columns(gathered, xh, 1 - c).astype(jnp.bfloat16), "c", SWAP)
-    numerators = columns(gathered, xh, c) + near_in.astype(jnp.float32) + far.astype(jnp.float32)
+    out = contract(gathered, tables[:2], jnp.bfloat16)
+    beside_in = lax.ppermute(out, "c", SWAP)
+    sums = contract(gathered, tables[2:], jnp.float32)
+    far = (sums[0] + beside_in[0].astype(jnp.float32)).astype(jnp.bfloat16)
+    far_in = lax.ppermute(far, "xh", SWAP)
+    numerators = sums[1] + beside_in[1].astype(jnp.float32) + far_in.astype(jnp.float32)
     energies = -(numerators * numerators) / energy_gap
     return (numerators, energies)
 

time: 102 us -> 95.4 us (0.935)
  matrix products: 13.1 us -> 3.26 us
  local copies, waits for them, and re-layouts: 2.75 us -> 11.2 us
  starting transfers between devices: 53.4 us -> 48.2 us
  waiting for transfers between devices: 27.5 us -> 24.5 us
  Pallas kernels: 0 us -> 2.78 us
    dot_general x4 -> x0, matrix products: 9.84 us -> none  [columns(): jnp.einsum('qtb,qbc->tc', rows, block, preferred_element_type=jnp.float32)]
    all_to_all x1, waiting for transfers between devices: 15.2 us -> 8.36 us  [shards(): own = lax.all_to_all(spread, FAR, 0, 0, tiled=True).reshape(192, width)]
    dynamic_slice x0 -> x1, local copies, waits for them, and re-layouts: none -> 6.82 us  [shards(): lax.dynamic_slice_in_dim(couplings, (h * 2 + k) * width, width, 2)]
    ppermute x3 -> x2, starting transfers between devices: 12.7 us -> 8.63 us  [the longest x1 4.36 us: shards(): far_in = lax.ppermute(far, 'xh', SWAP)]
    pallas_call x0 -> x2, Pallas kernels: none -> 2.78 us  [contract(): pl.pallas_call(contract_kernel, out_shape=jax.ShapeDtypeStruct((parts, ti...]
    ppermute x3, starting transfers between devices: 10.7 us -> 8.99 us  [shards(): lax.ppermute(own, NAMES, shift(0, *at))]
    ppermute x3, waiting for transfers between devices: 3.94 us -> 5.6 us  [shards(): lax.ppermute(beside, NAMES, shift(0, *at))]
    unnamed x3 -> x9, local copies, waits for them, and re-layouts: 0.52 us -> 2.19 us
  transfers between devices with their start and end apart: 11 -> 10, of which waited for: 6 -> 5; matrix products, arithmetic and copies ran while one was open for 8% -> 14% of each run, Pallas kernels for 0% -> 1%
where the time goes in v4:
time: 95.4 us; the launch traced here: 94.7 us
  starting transfers between devices  48.2 us (51%)
  waiting for transfers between devices  24.5 us (26%)
  local copies, waits for them, and re-layouts  11.2 us (12%)
  other arithmetic  3.66 us (4%)
  matrix products  3.26 us (3%)
  Pallas kernels  2.78 us (3%)
  between operations  1.01 us (1%)
    all_to_all x1, starting transfers between devices, shards(): own = lax.all_to_all(spread, FAR, 0, 0, tiled=True).reshape(192, width)  20.6 us
    ppermute x1, waiting for transfers between devices, shards(): far_in = lax.ppermute(far, 'xh', SWAP)  9.36 us
    ppermute x3, starting transfers between devices, shards(): lax.ppermute(own, NAMES, shift(0, *at))  8.99 us
    all_to_all x1, waiting for transfers between devices, shards(): own = lax.all_to_all(spread, FAR, 0, 0, tiled=True).reshape(192, width)  8.36 us
    ppermute x3, starting transfers between devices, shards(): lax.ppermute(beside, NAMES, shift(0, *at))  6.88 us
    dynamic_slice x1, local copies, waits for them, and re-layouts, shards(): lax.dynamic_slice_in_dim(couplings, (h * 2 + k) * width, width, 2)  6.82 us
    ppermute x3, waiting for transfers between devices, shards(): lax.ppermute(beside, NAMES, shift(0, *at))  5.6 us
    ppermute x1, starting transfers between devices, shards(): far_in = lax.ppermute(far, 'xh', SWAP)  4.36 us
  transfers between devices with their start and end apart: 10, of which 5 were waited for; matrix products, arithmetic and copies ran while one was open for 14% of the time, Pallas kernels for 1%

profile of v4, /device:TPU:1, one launch (start us, length us, event | category | flops | bytes accessed | tf_op | source)
XLA Modules:
  0.0 94.7 jit_solution(7708491357111296640)
XLA Ops:
  0.6 1.4 %broadcast_in_dim.7 = bf16[24,8,768]{2,1,0:T(8,128)(2,1)} broadcast(bf16[8,768]{1,0:T(8,128)(2,1)} %param.6), dimensions={1,2} | broadcast | bytes 307200 | tf_op jit(solution)/shard_map/broadcast_in_dim | solution.py:66
  2.1 20.6 %all-to-all-start = ((bf16[24,8,768]{2,1,0:T(8,128)(2,1)}), bf16[24,8,768]{2,1,0:T(8,128)(2,1)S(1)}, u32[]{:S(2)}, u32[]{:S(2)}) async-start(bf16[24,8,768]{2,1,0:T(8,128)(2,1)} %broadcast_in_dim.7), calls=%async_computation | async-start | bytes 589824 | tf_op jit(solution)/shard_map/all_to_all | solution.py:67
  22.7 0.5 broadcast.20
  23.2 1.3 %reduce.5 = s32[192]{0:T(256)S(1)} reduce(s32[1,192]{1,0:T(1,128)} %param.9, s32[]{:T(128)} %broadcast.20), dimensions={0}, to_apply=%param.9.reduce_sub_computation.3 | reduce | bytes 1540 | tf_op args[3]
  24.6 0.2 lt.127
  24.7 0.3 copy.8
  25.0 0.7 add_reduce_fusion
  25.8 0.2 add.157
  26.0 0.1 fusion.20
  26.1 0.1 reshape.39
  26.3 6.8 %constant_dynamic-slice_fusion.7 = (bf16[2,768,768]{2,1,0:T(8,128)(2,1)S(1)}, bf16[2,768,768]{2,1,0:T(8,128)(2,1)}, bf16[2,768,768]{2,1,0:T(8,128)(2,1)}, bf16[2,768,768]{2,1,0:T(8,128)(2,1)}) fusion(bf16[2,768,3072]{2,1,0:T(8,128)(2,1)} %param.10, s32[]{:T(128)S(6)} %select_n.126, s32[]{:T(128)S(6)} %select_n.124, s32[]{:T(128)S(6)} %select_n.123, ...), kind=kLoop, calls=%fused_computation.43 | loop fusion | bytes 18874384 | tf_op jit(solution)/shard_map/dynamic_slice | solution.py:69
  33.1 8.4 %all-to-all-done = bf16[24,8,768]{2,1,0:T(8,128)(2,1)S(1)} async-done(((bf16[24,8,768]{2,1,0:T(8,128)(2,1)}), bf16[24,8,768]{2,1,0:T(8,128)(2,1)S(1)}, u32[]{:S(2)}, u32[]{:S(2)}) %all-to-all-start) | async-done | bytes 294944 | tf_op jit(solution)/shard_map/all_to_all | solution.py:67
  41.4 3.1 %collective-permute-start.3 = (bf16[192,768]{1,0:T(8,128)(2,1)S(1)}, bf16[192,768]{1,0:T(8,128)(2,1)S(1)}, u32[]{:S(2)}, u32[]{:S(2)}) collective-permute-start(bf16[192,768]{1,0:T(8,128)(2,1)S(1)} %bitcast.26), channel_id=1, source_target_pairs={{0,384},{1,385},{2,386},{3,387},{4,388},{5,389},{6,390},{7,391},{8... | collective-permute-start | bytes 884744 | tf_op jit(solution)/shard_map/ppermute | solution.py:74
  44.6 4.9 %collective-permute-start.2 = (bf16[192,768]{1,0:T(8,128)(2,1)S(1)}, bf16[192,768]{1,0:T(8,128)(2,1)S(1)}, u32[]{:S(2)}, u32[]{:S(2)}) collective-permute-start(bf16[192,768]{1,0:T(8,128)(2,1)S(1)} %bitcast.27), channel_id=1, source_target_pairs={{0,380},{1,37},{2,382},{3,39},{4,352},{5,41},{6,354},{7,43},{8,356... | collective-permute-start | bytes 884744 | tf_op jit(solution)/shard_map/ppermute | solution.py:76
  49.5 1.9 %collective-permute-start.1 = (bf16[192,768]{1,0:T(8,128)(2,1)S(1)}, bf16[192,768]{1,0:T(8,128)(2,1)S(1)}, u32[]{:S(2)}, u32[]{:S(2)}) collective-permute-start(bf16[192,768]{1,0:T(8,128)(2,1)S(1)} %bitcast.28), channel_id=1, source_target_pairs={{0,352},{1,33},{2,354},{3,35},{4,356},{5,37},{6,358},{7,39},{8,360... | collective-permute-start | bytes 884744 | tf_op jit(solution)/shard_map/ppermute | solution.py:76
  51.4 2.2 %collective-permute-start = (bf16[192,768]{1,0:T(8,128)(2,1)S(1)}, bf16[192,768]{1,0:T(8,128)(2,1)S(1)}, u32[]{:S(2)}, u32[]{:S(2)}) collective-permute-start(bf16[192,768]{1,0:T(8,128)(2,1)S(1)} %bitcast.29), channel_id=1, source_target_pairs={{0,28},{1,5},{2,30},{3,7},{4,0},{5,9},{6,2},{7,11},{8,4},{9,13},{1... | collective-permute-start | bytes 884744 | tf_op jit(solution)/shard_map/ppermute | solution.py:76
  53.6 0.4 fusion.3
  54.0 0.0 collective-permute-done.3
  54.0 3.0 %collective-permute-start.6 = (bf16[192,768]{1,0:T(8,128)(2,1)S(1)}, bf16[192,768]{1,0:T(8,128)(2,1)S(1)}, u32[]{:S(2)}, u32[]{:S(2)}) collective-permute-start(bf16[192,768]{1,0:T(8,128)(2,1)S(1)} %collective-permute-done.3), channel_id=1, source_target_pairs={{0,380},{1,37},{2,382},{3,39},{4,352},{5,41},{6,354},{7,43},{8,356... | collective-permute-start | bytes 884744 | tf_op jit(solution)/shard_map/ppermute | solution.py:78
  57.0 1.9 %collective-permute-start.5 = (bf16[192,768]{1,0:T(8,128)(2,1)S(1)}, bf16[192,768]{1,0:T(8,128)(2,1)S(1)}, u32[]{:S(2)}, u32[]{:S(2)}) collective-permute-start(bf16[192,768]{1,0:T(8,128)(2,1)S(1)} %collective-permute-done.3), channel_id=1, source_target_pairs={{0,352},{1,33},{2,354},{3,35},{4,356},{5,37},{6,358},{7,39},{8,360... | collective-permute-start | bytes 884744 | tf_op jit(solution)/shard_map/ppermute | solution.py:78
  59.0 0.4 fusion.7
  59.4 0.7 collective-permute-done
  60.1 1.9 %collective-permute-start.4 = (bf16[192,768]{1,0:T(8,128)(2,1)S(1)}, bf16[192,768]{1,0:T(8,128)(2,1)S(1)}, u32[]{:S(2)}, u32[]{:S(2)}) collective-permute-start(bf16[192,768]{1,0:T(8,128)(2,1)S(1)} %collective-permute-done.3), channel_id=1, source_target_pairs={{0,28},{1,5},{2,30},{3,7},{4,0},{5,9},{6,2},{7,11},{8,4},{9,13},{1... | collective-permute-start | bytes 884744 | tf_op jit(solution)/shard_map/ppermute | solution.py:78
  62.0 0.4 fusion.4
  62.4 0.0 collective-permute-done.1
  62.4 0.4 fusion.5
  62.8 0.0 collective-permute-done.2
  62.8 0.4 fusion.6
  63.2 5.6 %collective-permute-done.4 = bf16[192,768]{1,0:T(8,128)(2,1)S(1)} collective-permute-done((bf16[192,768]{1,0:T(8,128)(2,1)S(1)}, bf16[192,768]{1,0:T(8,128)(2,1)S(1)}, u32[]{:S(2)}, u32[]{:S(2)}) %collective-permute-start.4) | collective-permute-done | bytes 294944 | tf_op jit(solution)/shard_map/ppermute | solution.py:78
  68.8 0.4 fusion.8
  69.1 0.0 collective-permute-done.5
  69.1 0.4 fusion.9
  69.5 0.0 collective-permute-done.6
  69.5 0.0 copy-start.1
  69.5 0.0 copy-start.2
  69.5 0.7 add_convert_fusion.rows_ref
  70.2 0.9 %copy-done.1 = bf16[2,768,768]{2,1,0:T(8,128)(2,1)S(1)} copy-done((bf16[2,768,768]{2,1,0:T(8,128)(2,1)S(1)}, bf16[2,768,768]{2,1,0:T(8,128)(2,1)}, u32[]{:S(2)}) %copy-start.1) | copy-done | bytes 2359320
  71.2 0.7 copy-done.2
  71.9 0.0 copy-start
  71.9 1.4 %shard_map.78 = bf16[2,256,768]{2,1,0:T(8,128)(2,1)S(1)} custom-call(bf16[512,768]{1,0:T(8,128)(2,1)S(1)} %add_convert_fusion.rows_ref, bf16[2,768,768]{2,1,0:T(8,128)(2,1)S(1)} %copy-done.2, bf16[2,768,768]{2,1,0:T(8,128)(2,1)S(1)} %copy-done.1), custom_call_target="tpu_custom_call" | custom-call | flops 1207959552 | bytes 4718592 | tf_op jit(solution)/shard_map/pallas_call | solution.py:47
  73.3 4.3 %collective-permute-start.7 = (bf16[2,256,768]{2,1,0:T(8,128)(2,1)S(1)}, bf16[2,256,768]{2,1,0:T(8,128)(2,1)S(1)}, u32[]{:S(2)}, u32[]{:S(2)}) collective-permute-start(bf16[2,256,768]{2,1,0:T(8,128)(2,1)S(1)} %shard_map.78), channel_id=1, source_target_pairs={{0,1},{1,0},{2,3},{3,2},{4,5},{5,4},{6,7},{7,6},{8,9},{9,8},{10,11... | collective-permute-start | bytes 2359304 | tf_op jit(solution)/shard_map/ppermute | solution.py:96
  77.6 0.0 copy-done
  77.6 1.4 %shard_map.77 = f32[2,256,768]{2,1,0:T(8,128)S(1)} custom-call(bf16[512,768]{1,0:T(8,128)(2,1)S(1)} %add_convert_fusion.rows_ref, bf16[2,768,768]{2,1,0:T(8,128)(2,1)S(1)} %copy-done, bf16[2,768,768]{2,1,0:T(8,128)(2,1)S(1)} %get-tuple-element.9.refs_1_), custom_call_target="tpu_custom_call" | custom-call | flops 1207959552 | bytes 4718592 | tf_op jit(solution)/shard_map/pallas_call | solution.py:47
  79.0 0.0 copy-start.3
  79.0 0.5 collective-permute-done.7
  79.5 0.1 fusion.11
  79.6 4.4 %collective-permute-start.8 = (bf16[256,768]{1,0:T(8,128)(2,1)S(1)}, bf16[256,768]{1,0:T(8,128)(2,1)S(1)}, u32[]{:S(2)}, u32[]{:S(2)}) collective-permute-start(bf16[256,768]{1,0:T(8,128)(2,1)S(1)} %fusion.11), channel_id=1, source_target_pairs={{0,2},{2,0},{1,3},{3,1},{4,6},{6,4},{5,7},{7,5},{8,10},{10,8},{9,1... | collective-permute-start | bytes 1179656 | tf_op jit(solution)/shard_map/ppermute | solution.py:99
  83.9 9.4 %collective-permute-done.8 = bf16[256,768]{1,0:T(8,128)(2,1)S(1)} collective-permute-done((bf16[256,768]{1,0:T(8,128)(2,1)S(1)}, bf16[256,768]{1,0:T(8,128)(2,1)S(1)}, u32[]{:S(2)}, u32[]{:S(2)}) %collective-permute-start.8) | collective-permute-done | bytes 393248 | tf_op jit(solution)/shard_map/ppermute | solution.py:99
  93.3 0.0 copy-done.3
  93.3 1.4 %negate_divide_fusion = (f32[256,768]{1,0:T(8,128)}, f32[256,768]{1,0:T(8,128)}) fusion(f32[256,768]{1,0:T(8,128)S(1)} %copy-done.3, bf16[256,768]{1,0:T(8,128)(2,1)S(1)} %collective-permute-done.8, bf16[2,256,768]{2,1,0:T(8,128)(2,1)S(1)} %collective-permute-done.7, f32[2,256,768]{2,1,0:T(8,128)S(1)} %shard_map.77), kind=kLoop, calls=%fused_computation.6 | loop fusion | flops 1376256 | bytes 3932160 | tf_op jit(solution)/shard_map/div | solution.py:101
  (1 shorter events, 0.0 us)
Async XLA Ops:
  2.1 39.4 %all-to-all-start = ((bf16[24,8,768]{2,1,0:T(8,128)(2,1)}), bf16[24,8,768]{2,1,0:T(8,128)(2,1)S(1)}, u32[]{:S(2)}, u32[]{:S(2)}) async-start(bf16[24,8,768]{2,1,0:T(8,128)(2,1)} %broadcast_in_dim.7), calls=%async_computation | async-start | bytes 589824 | tf_op jit(solution)/shard_map/all_to_all | solution.py:67
  41.4 12.5 %collective-permute-start.3 = (bf16[192,768]{1,0:T(8,128)(2,1)S(1)}, bf16[192,768]{1,0:T(8,128)(2,1)S(1)}, u32[]{:S(2)}, u32[]{:S(2)}) collective-permute-start(bf16[192,768]{1,0:T(8,128)(2,1)S(1)} %bitcast.26), channel_id=1, source_target_pairs={{0,384},{1,385},{2,386},{3,387},{4,388},{5,389},{6,390},{7,391},{8... | collective-permute-start | bytes 884744 | tf_op jit(solution)/shard_map/ppermute | solution.py:74
  44.6 18.2 %collective-permute-start.2 = (bf16[192,768]{1,0:T(8,128)(2,1)S(1)}, bf16[192,768]{1,0:T(8,128)(2,1)S(1)}, u32[]{:S(2)}, u32[]{:S(2)}) collective-permute-start(bf16[192,768]{1,0:T(8,128)(2,1)S(1)} %bitcast.27), channel_id=1, source_target_pairs={{0,380},{1,37},{2,382},{3,39},{4,352},{5,41},{6,354},{7,43},{8,356... | collective-permute-start | bytes 884744 | tf_op jit(solution)/shard_map/ppermute | solution.py:76
  49.5 12.9 %collective-permute-start.1 = (bf16[192,768]{1,0:T(8,128)(2,1)S(1)}, bf16[192,768]{1,0:T(8,128)(2,1)S(1)}, u32[]{:S(2)}, u32[]{:S(2)}) collective-permute-start(bf16[192,768]{1,0:T(8,128)(2,1)S(1)} %bitcast.28), channel_id=1, source_target_pairs={{0,352},{1,33},{2,354},{3,35},{4,356},{5,37},{6,358},{7,39},{8,360... | collective-permute-start | bytes 884744 | tf_op jit(solution)/shard_map/ppermute | solution.py:76
  51.4 8.7 %collective-permute-start = (bf16[192,768]{1,0:T(8,128)(2,1)S(1)}, bf16[192,768]{1,0:T(8,128)(2,1)S(1)}, u32[]{:S(2)}, u32[]{:S(2)}) collective-permute-start(bf16[192,768]{1,0:T(8,128)(2,1)S(1)} %bitcast.29), channel_id=1, source_target_pairs={{0,28},{1,5},{2,30},{3,7},{4,0},{5,9},{6,2},{7,11},{8,4},{9,13},{1... | collective-permute-start | bytes 884744 | tf_op jit(solution)/shard_map/ppermute | solution.py:76
  54.0 15.5 %collective-permute-start.6 = (bf16[192,768]{1,0:T(8,128)(2,1)S(1)}, bf16[192,768]{1,0:T(8,128)(2,1)S(1)}, u32[]{:S(2)}, u32[]{:S(2)}) collective-permute-start(bf16[192,768]{1,0:T(8,128)(2,1)S(1)} %collective-permute-done.3), channel_id=1, source_target_pairs={{0,380},{1,37},{2,382},{3,39},{4,352},{5,41},{6,354},{7,43},{8,356... | collective-permute-start | bytes 884744 | tf_op jit(solution)/shard_map/ppermute | solution.py:78
  57.0 12.1 %collective-permute-start.5 = (bf16[192,768]{1,0:T(8,128)(2,1)S(1)}, bf16[192,768]{1,0:T(8,128)(2,1)S(1)}, u32[]{:S(2)}, u32[]{:S(2)}) collective-permute-start(bf16[192,768]{1,0:T(8,128)(2,1)S(1)} %collective-permute-done.3), channel_id=1, source_target_pairs={{0,352},{1,33},{2,354},{3,35},{4,356},{5,37},{6,358},{7,39},{8,360... | collective-permute-start | bytes 884744 | tf_op jit(solution)/shard_map/ppermute | solution.py:78
  60.1 8.7 %collective-permute-start.4 = (bf16[192,768]{1,0:T(8,128)(2,1)S(1)}, bf16[192,768]{1,0:T(8,128)(2,1)S(1)}, u32[]{:S(2)}, u32[]{:S(2)}) collective-permute-start(bf16[192,768]{1,0:T(8,128)(2,1)S(1)} %collective-permute-done.3), channel_id=1, source_target_pairs={{0,28},{1,5},{2,30},{3,7},{4,0},{5,9},{6,2},{7,11},{8,4},{9,13},{1... | collective-permute-start | bytes 884744 | tf_op jit(solution)/shard_map/ppermute | solution.py:78
  69.5 1.7 %copy-start.1 = (bf16[2,768,768]{2,1,0:T(8,128)(2,1)S(1)}, bf16[2,768,768]{2,1,0:T(8,128)(2,1)}, u32[]{:S(2)}) copy-start(bf16[2,768,768]{2,1,0:T(8,128)(2,1)} %get-tuple-element.11.refs_1_) | copy-start | bytes 7077892
  69.5 2.4 %copy-start.2 = (bf16[2,768,768]{2,1,0:T(8,128)(2,1)S(1)}, bf16[2,768,768]{2,1,0:T(8,128)(2,1)}, u32[]{:S(2)}) copy-start(bf16[2,768,768]{2,1,0:T(8,128)(2,1)} %get-tuple-element.10.refs_0_) | copy-start | bytes 7077892
  71.9 5.7 %copy-start = (bf16[2,768,768]{2,1,0:T(8,128)(2,1)S(1)}, bf16[2,768,768]{2,1,0:T(8,128)(2,1)}, u32[]{:S(2)}) copy-start(bf16[2,768,768]{2,1,0:T(8,128)(2,1)} %get-tuple-element.8.refs_0_) | copy-start | bytes 7077892
  73.3 6.2 %collective-permute-start.7 = (bf16[2,256,768]{2,1,0:T(8,128)(2,1)S(1)}, bf16[2,256,768]{2,1,0:T(8,128)(2,1)S(1)}, u32[]{:S(2)}, u32[]{:S(2)}) collective-permute-start(bf16[2,256,768]{2,1,0:T(8,128)(2,1)S(1)} %shard_map.78), channel_id=1, source_target_pairs={{0,1},{1,0},{2,3},{3,2},{4,5},{5,4},{6,7},{7,6},{8,9},{9,8},{10,11... | collective-permute-start | bytes 2359304 | tf_op jit(solution)/shard_map/ppermute | solution.py:96
  79.0 14.3 %copy-start.3 = (f32[256,768]{1,0:T(8,128)S(1)}, f32[256,768]{1,0:T(8,128)}, u32[]{:S(2)}) copy-start(f32[256,768]{1,0:T(8,128)} %param.11) | copy-start | bytes 2359300
  79.6 13.7 %collective-permute-start.8 = (bf16[256,768]{1,0:T(8,128)(2,1)S(1)}, bf16[256,768]{1,0:T(8,128)(2,1)S(1)}, u32[]{:S(2)}, u32[]{:S(2)}) collective-permute-start(bf16[256,768]{1,0:T(8,128)(2,1)S(1)} %fusion.11), channel_id=1, source_target_pairs={{0,2},{2,0},{1,3},{3,1},{4,6},{6,4},{5,7},{7,5},{8,10},{10,8},{9,1... | collective-permute-start | bytes 1179656 | tf_op jit(solution)/shard_map/ppermute | solution.py:99

commit v5 on v4

--- a/solution.py
+++ b/solution.py
@@ -21,33 +21,48 @@
             for y in range(8):
                 for k in range(4):
                     s = 1 if k % 2 else -1
-                    there = (((x + dx) % 2) * 12 + (z + s * dz) % 12) * 8 + (y + s * dy) % 8
+                    there = (((x + dx) % 2) * 12 + (z + s * dz) % 12) * 8 + (y - s * dy) % 8
                     pairs.append((((x * 12 + z) * 8 + y) * 4 + k, there * 4 + k))
     return pairs
 
 
-def contract_kernel(rows_ref, *refs):
-    tables, out_ref = refs[:-1], refs[-1]
-    tile_rows = out_ref.shape[1]
-    for p, table_ref in enumerate(tables):
-        total = None
-        for q in range(table_ref.shape[0]):
-            term = jnp.dot(
-                rows_ref[q * tile_rows:(q + 1) * tile_rows, :],
-                table_ref[q],
-                preferred_element_type=jnp.float32,
-            )
-            total = term if total is None else total + term
-        out_ref[p] = total.astype(out_ref.dtype)
+def product(rows_ref, read, blocks, tile_rows):
+    total = None
+    for q in range(blocks):
+        term = jnp.dot(
+            rows_ref[q * tile_rows:(q + 1) * tile_rows, :],
+            read(q),
+            preferred_element_type=jnp.float32,
+        )
+        total = term if total is None else total + term
+    return total
 
 
-def contract(rows, tables, kind):
-    blocks, depth, width = tables[0].shape
-    parts, tile_rows = len(tables), rows.shape[0] // blocks
+def columns_kernel(starts, rows_ref, table_ref, out_ref):
+    parts, tile_rows, width = out_ref.shape
+    for p in range(parts):
+        at = pl.ds(pl.multiple_of(starts[p], 128), width)
+        out = product(rows_ref, lambda q: table_ref[q, :, at], table_ref.shape[0], tile_rows)
+        out_ref[p] = out.astype(out_ref.dtype)
+
+
+def tables_kernel(rows_ref, *refs):
+    tables, out_ref = refs[:-1], refs[-1]
+    for p, table_ref in enumerate(tables):
+        out = product(rows_ref, lambda q: table_ref[q], table_ref.shape[0], out_ref.shape[1])
+        out_ref[p] = out.astype(out_ref.dtype)
+
+
+def contract(kernel, starts, rows, tables, kind):
+    blocks, depth, _ = tables[0].shape
+    parts = len(tables) if starts is None else starts.shape[0]
+    tile_rows, width = rows.shape[0] // blocks, rows.shape[1]
+    scalars = [] if starts is None else [starts]
     return pl.pallas_call(
-        contract_kernel,
+        kernel,
         out_shape=jax.ShapeDtypeStruct((parts, tile_rows, width), kind),
-        in_specs=[pl.BlockSpec(memory_space=pltpu.VMEM) for _ in range(1 + parts)],
+        in_specs=[pl.BlockSpec(memory_space=pltpu.SMEM) for _ in scalars]
+        + [pl.BlockSpec(memory_space=pltpu.VMEM) for _ in range(1 + len(tables))],
         out_specs=pl.BlockSpec(memory_space=pltpu.VMEM),
         compiler_params=pltpu.CompilerParams(vmem_limit_bytes=20 << 20),
         cost_estimate=pl.CostEstimate(
@@ -55,7 +70,7 @@
             bytes_accessed=2 * parts * blocks * depth * width,
             transcendentals=0,
         ),
-    )(rows, *tables)
+    )(*scalars, rows, *tables)
 
 
 def shards(core_coef, dest_rows, block_ids, bin_offsets, couplings, energy_gap):
@@ -66,16 +81,15 @@
     spread = jnp.broadcast_to(core_coef[None], (24, group_rows, width))
     own = lax.all_to_all(spread, FAR, 0, 0, tiled=True).reshape(192, width)
     tables = [
-        lax.dynamic_slice_in_dim(couplings, (h * 2 + k) * width, width, 2)
-        for k in (1 - c, c)
-        for h in (1 - xh, xh)
+        lax.dynamic_slice_in_dim(couplings, (h * 2 + c) * width, width, 2) for h in (1 - xh, xh)
     ]
     own, tables = lax.optimization_barrier((own, tables))
     beside = lax.ppermute(own, NAMES, shift(1, 0, 0))
-    pieces = [((0, 0, 0), own)]
-    pieces += [((0,) + at, lax.ppermute(own, NAMES, shift(0, *at))) for at in NEAR]
+    across = [lax.ppermute(own, NAMES, shift(0, *at)) for at in NEAR]
+    pieces = [((0, 0, 0), own)] + [((0,) + at, piece) for at, piece in zip(NEAR, across)]
     pieces += [((1, 0, 0), beside)]
-    pieces += [((1,) + at, lax.ppermute(beside, NAMES, shift(0, *at))) for at in NEAR]
+    pieces += [((1,) + at, lax.ppermute(beside, NAMES, shift(0, *at))) for at in NEAR[:2]]
+    pieces += [((1,) + NEAR[2], lax.ppermute(across[2], NAMES, shift(1, 0, 0)))]
 
     within = jnp.arange(8, dtype=jnp.int32)
     target = jnp.where(
@@ -92,9 +106,10 @@
         summed = summed + jnp.dot(onehot, piece, preferred_element_type=jnp.float32)
     gathered = summed.astype(jnp.bfloat16)
 
-    out = contract(gathered, tables[:2], jnp.bfloat16)
+    starts = jnp.stack([(h * 2 + 1 - c) * width for h in (1 - xh, xh)])
+    out = contract(columns_kernel, starts, gathered, [couplings], jnp.bfloat16)
     beside_in = lax.ppermute(out, "c", SWAP)
-    sums = contract(gathered, tables[2:], jnp.float32)
+    sums = contract(tables_kernel, None, gathered, tables, jnp.float32)
     far = (sums[0] + beside_in[0].astype(jnp.float32)).astype(jnp.bfloat16)
     far_in = lax.ppermute(far, "xh", SWAP)
     numerators = sums[1] + beside_in[1].astype(jnp.float32) + far_in.astype(jnp.float32)

time: 95.4 us -> 93.1 us (0.976)
  local copies, waits for them, and re-layouts: 11.2 us -> 7.44 us
  starting transfers between devices: 48.2 us -> 49.5 us
    ppermute x3 -> x2, waiting for transfers between devices: 5.6 us -> 1.89 us  [shards(): lax.ppermute(beside, NAMES, shift(0, *at))]
    dynamic_slice x1, local copies, waits for them, and re-layouts: 6.82 us -> 4.16 us  [shards(): lax.dynamic_slice_in_dim(couplings, (h * 2 + c) * width, width, 2)]
    all_to_all x1, waiting for transfers between devices: 8.36 us -> 11 us  [shards(): own = lax.all_to_all(spread, FAR, 0, 0, tiled=True).reshape(192, width)]
    ppermute x3 -> x2, starting transfers between devices: 6.88 us -> 4.69 us  [shards(): lax.ppermute(beside, NAMES, shift(0, *at))]
    ppermute x3 -> x4, starting transfers between devices: 8.99 us -> 10.8 us  [the longest x3 8.59 us: shards(): across = [lax.ppermute(own, NAMES, shift(0, *at)) for at in NEAR]]
    ppermute x1, starting transfers between devices: 4.27 us -> 6 us  [shards(): beside_in = lax.ppermute(out, 'c', SWAP)]
    unnamed x9 -> x11, local copies, waits for them, and re-layouts: 2.19 us -> 1.04 us
  transfers between devices with their start and end apart: 10 -> 10, of which waited for: 5 -> 5; matrix products, arithmetic and copies ran while one was open for 14% -> 11% of each run, Pallas kernels for 1% -> 1%
where the time goes in v5:
time: 93.1 us; the launch traced here: 92.4 us
  starting transfers between devices  49.5 us (53%)
  waiting for transfers between devices  24.1 us (26%)
  local copies, waits for them, and re-layouts  7.44 us (8%)
  other arithmetic  3.71 us (4%)
  Pallas kernels  3.36 us (4%)
  matrix products  3.26 us (4%)
  between operations  1.02 us (1%)
    all_to_all x1, starting transfers between devices, shards(): own = lax.all_to_all(spread, FAR, 0, 0, tiled=True).reshape(192, width)  20.6 us
    all_to_all x1, waiting for transfers between devices, shards(): own = lax.all_to_all(spread, FAR, 0, 0, tiled=True).reshape(192, width)  11 us
    ppermute x1, waiting for transfers between devices, shards(): far_in = lax.ppermute(far, 'xh', SWAP)  9.36 us
    ppermute x3, starting transfers between devices, shards(): across = [lax.ppermute(own, NAMES, shift(0, *at)) for at in NEAR]  8.59 us
    ppermute x1, starting transfers between devices, shards(): beside_in = lax.ppermute(out, 'c', SWAP)  6 us
    ppermute x2, starting transfers between devices, shards(): lax.ppermute(beside, NAMES, shift(0, *at))  4.69 us
    ppermute x1, starting transfers between devices, shards(): far_in = lax.ppermute(far, 'xh', SWAP)  4.36 us
    dynamic_slice x1, local copies, waits for them, and re-layouts, shards(): lax.dynamic_slice_in_dim(couplings, (h * 2 + c) * width, width, 2)  4.16 us
  transfers between devices with their start and end apart: 10, of which 5 were waited for; matrix products, arithmetic and copies ran while one was open for 11% of the time, Pallas kernels for 1%

profile of v5, /device:TPU:1, one launch (start us, length us, event | category | flops | bytes accessed | tf_op | source)
XLA Modules:
  0.0 92.4 jit_solution(7945640758676617732)
XLA Ops:
  0.6 1.4 %broadcast_in_dim.7 = bf16[24,8,768]{2,1,0:T(8,128)(2,1)} broadcast(bf16[8,768]{1,0:T(8,128)(2,1)} %param.6), dimensions={1,2} | broadcast | bytes 307200 | tf_op jit(solution)/shard_map/broadcast_in_dim | solution.py:81
  2.1 20.6 %all-to-all-start = ((bf16[24,8,768]{2,1,0:T(8,128)(2,1)}), bf16[24,8,768]{2,1,0:T(8,128)(2,1)S(1)}, u32[]{:S(2)}, u32[]{:S(2)}) async-start(bf16[24,8,768]{2,1,0:T(8,128)(2,1)} %broadcast_in_dim.7), calls=%async_computation | async-start | bytes 589824 | tf_op jit(solution)/shard_map/all_to_all | solution.py:82
  22.7 0.5 broadcast.20
  23.2 1.3 %reduce.5 = s32[192]{0:T(256)S(1)} reduce(s32[1,192]{1,0:T(1,128)} %param.9, s32[]{:T(128)} %broadcast.20), dimensions={0}, to_apply=%param.9.reduce_sub_computation.3 | reduce | bytes 1540 | tf_op args[3]
  24.6 0.2 lt.121
  24.7 0.3 copy.8
  25.0 0.7 add_reduce_fusion
  25.8 0.2 add.151
  26.0 0.1 fusion.20
  26.1 0.1 reshape.39
  26.3 4.2 %constant_dynamic-slice_fusion.7 = (bf16[2,768,768]{2,1,0:T(8,128)(2,1)S(1)}, bf16[2,768,768]{2,1,0:T(8,128)(2,1)}) fusion(bf16[2,768,3072]{2,1,0:T(8,128)(2,1)} %table_ref.1, s32[]{:T(128)S(6)} %select_n.118, s32[]{:T(128)S(6)} %select_n.117), kind=kLoop, calls=%fused_computation.43 | loop fusion | bytes 9437192 | tf_op jit(solution)/shard_map/dynamic_slice | solution.py:84
  30.5 11.0 %all-to-all-done = bf16[24,8,768]{2,1,0:T(8,128)(2,1)S(1)} async-done(((bf16[24,8,768]{2,1,0:T(8,128)(2,1)}), bf16[24,8,768]{2,1,0:T(8,128)(2,1)S(1)}, u32[]{:S(2)}, u32[]{:S(2)}) %all-to-all-start) | async-done | bytes 294944 | tf_op jit(solution)/shard_map/all_to_all | solution.py:82
  41.4 3.1 %collective-permute-start.3 = (bf16[192,768]{1,0:T(8,128)(2,1)S(1)}, bf16[192,768]{1,0:T(8,128)(2,1)S(1)}, u32[]{:S(2)}, u32[]{:S(2)}) collective-permute-start(bf16[192,768]{1,0:T(8,128)(2,1)S(1)} %bitcast.30), channel_id=1, source_target_pairs={{0,384},{1,385},{2,386},{3,387},{4,388},{5,389},{6,390},{7,391},{8... | collective-permute-start | bytes 884744 | tf_op jit(solution)/shard_map/ppermute | solution.py:87
  44.6 3.4 %collective-permute-start.2 = (bf16[192,768]{1,0:T(8,128)(2,1)S(1)}, bf16[192,768]{1,0:T(8,128)(2,1)S(1)}, u32[]{:S(2)}, u32[]{:S(2)}) collective-permute-start(bf16[192,768]{1,0:T(8,128)(2,1)S(1)} %bitcast.31), channel_id=1, source_target_pairs={{0,356},{1,61},{2,358},{3,63},{4,360},{5,33},{6,362},{7,35},{8,364... | collective-permute-start | bytes 884744 | tf_op jit(solution)/shard_map/ppermute | solution.py:88
  47.9 0.1 pad_add_fusion.starts
  48.0 3.3 %collective-permute-start.1 = (bf16[192,768]{1,0:T(8,128)(2,1)S(1)}, bf16[192,768]{1,0:T(8,128)(2,1)S(1)}, u32[]{:S(2)}, u32[]{:S(2)}) collective-permute-start(bf16[192,768]{1,0:T(8,128)(2,1)S(1)} %bitcast.32), channel_id=1, source_target_pairs={{0,352},{1,33},{2,354},{3,35},{4,356},{5,37},{6,358},{7,39},{8,360... | collective-permute-start | bytes 884744 | tf_op jit(solution)/shard_map/ppermute | solution.py:88
  51.3 1.9 %collective-permute-start = (bf16[192,768]{1,0:T(8,128)(2,1)S(1)}, bf16[192,768]{1,0:T(8,128)(2,1)S(1)}, u32[]{:S(2)}, u32[]{:S(2)}) collective-permute-start(bf16[192,768]{1,0:T(8,128)(2,1)S(1)} %bitcast.33), channel_id=1, source_target_pairs={{0,4},{1,29},{2,6},{3,31},{4,8},{5,1},{6,10},{7,3},{8,12},{9,5},{1... | collective-permute-start | bytes 884744 | tf_op jit(solution)/shard_map/ppermute | solution.py:88
  53.3 0.4 fusion.3
  53.6 0.0 collective-permute-done.3
  53.6 2.5 %collective-permute-start.5 = (bf16[192,768]{1,0:T(8,128)(2,1)S(1)}, bf16[192,768]{1,0:T(8,128)(2,1)S(1)}, u32[]{:S(2)}, u32[]{:S(2)}) collective-permute-start(bf16[192,768]{1,0:T(8,128)(2,1)S(1)} %collective-permute-done.3), channel_id=1, source_target_pairs={{0,352},{1,33},{2,354},{3,35},{4,356},{5,37},{6,358},{7,39},{8,360... | collective-permute-start | bytes 884744 | tf_op jit(solution)/shard_map/ppermute | solution.py:91
  56.2 2.2 %collective-permute-start.4 = (bf16[192,768]{1,0:T(8,128)(2,1)S(1)}, bf16[192,768]{1,0:T(8,128)(2,1)S(1)}, u32[]{:S(2)}, u32[]{:S(2)}) collective-permute-start(bf16[192,768]{1,0:T(8,128)(2,1)S(1)} %collective-permute-done.3), channel_id=1, source_target_pairs={{0,4},{1,29},{2,6},{3,31},{4,8},{5,1},{6,10},{7,3},{8,12},{9,5},{1... | collective-permute-start | bytes 884744 | tf_op jit(solution)/shard_map/ppermute | solution.py:91
  58.4 0.0 collective-permute-done.2
  58.4 2.2 %collective-permute-start.6 = (bf16[192,768]{1,0:T(8,128)(2,1)S(1)}, bf16[192,768]{1,0:T(8,128)(2,1)S(1)}, u32[]{:S(2)}, u32[]{:S(2)}) collective-permute-start(bf16[192,768]{1,0:T(8,128)(2,1)S(1)} %collective-permute-done.2), channel_id=1, source_target_pairs={{0,384},{1,385},{2,386},{3,387},{4,388},{5,389},{6,390},{7,391},{8... | collective-permute-start | bytes 884744 | tf_op jit(solution)/shard_map/ppermute | solution.py:92
  60.5 0.4 fusion.6
  60.9 0.0 slice-start
  60.9 0.4 fusion.7
  61.3 0.0 collective-permute-done
  61.3 0.4 fusion.4
  61.7 0.0 collective-permute-done.1
  61.7 0.4 fusion.5
  62.1 1.9 %collective-permute-done.4 = bf16[192,768]{1,0:T(8,128)(2,1)S(1)} collective-permute-done((bf16[192,768]{1,0:T(8,128)(2,1)S(1)}, bf16[192,768]{1,0:T(8,128)(2,1)S(1)}, u32[]{:S(2)}, u32[]{:S(2)}) %collective-permute-start.4) | collective-permute-done | bytes 294944 | tf_op jit(solution)/shard_map/ppermute | solution.py:91
  64.0 0.0 slice-start.1
  64.0 0.4 fusion.8
  64.3 0.0 collective-permute-done.5
  64.3 0.4 fusion.9
  64.7 1.4 %collective-permute-done.6 = bf16[192,768]{1,0:T(8,128)(2,1)S(1)} collective-permute-done((bf16[192,768]{1,0:T(8,128)(2,1)S(1)}, bf16[192,768]{1,0:T(8,128)(2,1)S(1)}, u32[]{:S(2)}, u32[]{:S(2)}) %collective-permute-start.6) | collective-permute-done | bytes 294944 | tf_op jit(solution)/shard_map/ppermute | solution.py:92
  66.1 0.0 slice-start.2
  66.1 0.7 add_convert_fusion.rows_ref
  66.8 0.0 slice-done
  66.8 0.0 slice-done.1
  66.8 0.5 slice-done.2
  67.4 0.0 copy-start
  67.4 2.0 %shard_map.78 = bf16[2,256,768]{2,1,0:T(8,128)(2,1)S(1)} custom-call(s32[2]{0:T(128)S(1)} %pad_add_fusion.starts, bf16[512,768]{1,0:T(8,128)(2,1)S(1)} %add_convert_fusion.rows_ref, bf16[2,768,3072]{2,1,0:T(8,128)(2,1)S(1)} %bitcast.29), custom_call_target="tpu_custom_call" | custom-call | flops 1207959552 | bytes 4718592 | tf_op jit(solution)/shard_map/pallas_call | solution.py:61
  69.3 6.0 %collective-permute-start.7 = (bf16[2,256,768]{2,1,0:T(8,128)(2,1)S(1)}, bf16[2,256,768]{2,1,0:T(8,128)(2,1)S(1)}, u32[]{:S(2)}, u32[]{:S(2)}) collective-permute-start(bf16[2,256,768]{2,1,0:T(8,128)(2,1)S(1)} %shard_map.78), channel_id=1, source_target_pairs={{0,1},{1,0},{2,3},{3,2},{4,5},{5,4},{6,7},{7,6},{8,9},{9,8},{10,11... | collective-permute-start | bytes 2359304 | tf_op jit(solution)/shard_map/ppermute | solution.py:111
  75.3 0.0 copy-done
  75.4 1.4 %shard_map.77 = f32[2,256,768]{2,1,0:T(8,128)S(1)} custom-call(bf16[512,768]{1,0:T(8,128)(2,1)S(1)} %add_convert_fusion.rows_ref, bf16[2,768,768]{2,1,0:T(8,128)(2,1)S(1)} %copy-done, bf16[2,768,768]{2,1,0:T(8,128)(2,1)S(1)} %get-tuple-element.7.refs_1_), custom_call_target="tpu_custom_call" | custom-call | flops 1207959552 | bytes 4718592 | tf_op jit(solution)/shard_map/pallas_call | solution.py:61
  76.7 0.0 copy-start.1
  76.8 0.5 collective-permute-done.7
  77.2 0.1 fusion.11
  77.3 4.4 %collective-permute-start.8 = (bf16[256,768]{1,0:T(8,128)(2,1)S(1)}, bf16[256,768]{1,0:T(8,128)(2,1)S(1)}, u32[]{:S(2)}, u32[]{:S(2)}) collective-permute-start(bf16[256,768]{1,0:T(8,128)(2,1)S(1)} %fusion.11), channel_id=1, source_target_pairs={{0,2},{2,0},{1,3},{3,1},{4,6},{6,4},{5,7},{7,5},{8,10},{10,8},{9,1... | collective-permute-start | bytes 1179656 | tf_op jit(solution)/shard_map/ppermute | solution.py:114
  81.7 9.4 %collective-permute-done.8 = bf16[256,768]{1,0:T(8,128)(2,1)S(1)} collective-permute-done((bf16[256,768]{1,0:T(8,128)(2,1)S(1)}, bf16[256,768]{1,0:T(8,128)(2,1)S(1)}, u32[]{:S(2)}, u32[]{:S(2)}) %collective-permute-start.8) | collective-permute-done | bytes 393248 | tf_op jit(solution)/shard_map/ppermute | solution.py:114
  91.0 0.0 copy-done.1
  91.0 1.4 %negate_divide_fusion = (f32[256,768]{1,0:T(8,128)}, f32[256,768]{1,0:T(8,128)}) fusion(f32[256,768]{1,0:T(8,128)S(1)} %copy-done.1, bf16[256,768]{1,0:T(8,128)(2,1)S(1)} %collective-permute-done.8, bf16[2,256,768]{2,1,0:T(8,128)(2,1)S(1)} %collective-permute-done.7, f32[2,256,768]{2,1,0:T(8,128)S(1)} %shard_map.77), kind=kLoop, calls=%fused_computation.6 | loop fusion | flops 1376256 | bytes 3932160 | tf_op jit(solution)/shard_map/div | solution.py:116
  (2 shorter events, 0.0 us)
Async XLA Ops:
  2.1 39.4 %all-to-all-start = ((bf16[24,8,768]{2,1,0:T(8,128)(2,1)}), bf16[24,8,768]{2,1,0:T(8,128)(2,1)S(1)}, u32[]{:S(2)}, u32[]{:S(2)}) async-start(bf16[24,8,768]{2,1,0:T(8,128)(2,1)} %broadcast_in_dim.7), calls=%async_computation | async-start | bytes 589824 | tf_op jit(solution)/shard_map/all_to_all | solution.py:82
  41.4 12.2 %collective-permute-start.3 = (bf16[192,768]{1,0:T(8,128)(2,1)S(1)}, bf16[192,768]{1,0:T(8,128)(2,1)S(1)}, u32[]{:S(2)}, u32[]{:S(2)}) collective-permute-start(bf16[192,768]{1,0:T(8,128)(2,1)S(1)} %bitcast.30), channel_id=1, source_target_pairs={{0,384},{1,385},{2,386},{3,387},{4,388},{5,389},{6,390},{7,391},{8... | collective-permute-start | bytes 884744 | tf_op jit(solution)/shard_map/ppermute | solution.py:87
  44.6 13.8 %collective-permute-start.2 = (bf16[192,768]{1,0:T(8,128)(2,1)S(1)}, bf16[192,768]{1,0:T(8,128)(2,1)S(1)}, u32[]{:S(2)}, u32[]{:S(2)}) collective-permute-start(bf16[192,768]{1,0:T(8,128)(2,1)S(1)} %bitcast.31), channel_id=1, source_target_pairs={{0,356},{1,61},{2,358},{3,63},{4,360},{5,33},{6,362},{7,35},{8,364... | collective-permute-start | bytes 884744 | tf_op jit(solution)/shard_map/ppermute | solution.py:88
  48.0 13.7 %collective-permute-start.1 = (bf16[192,768]{1,0:T(8,128)(2,1)S(1)}, bf16[192,768]{1,0:T(8,128)(2,1)S(1)}, u32[]{:S(2)}, u32[]{:S(2)}) collective-permute-start(bf16[192,768]{1,0:T(8,128)(2,1)S(1)} %bitcast.32), channel_id=1, source_target_pairs={{0,352},{1,33},{2,354},{3,35},{4,356},{5,37},{6,358},{7,39},{8,360... | collective-permute-start | bytes 884744 | tf_op jit(solution)/shard_map/ppermute | solution.py:88
  51.3 10.0 %collective-permute-start = (bf16[192,768]{1,0:T(8,128)(2,1)S(1)}, bf16[192,768]{1,0:T(8,128)(2,1)S(1)}, u32[]{:S(2)}, u32[]{:S(2)}) collective-permute-start(bf16[192,768]{1,0:T(8,128)(2,1)S(1)} %bitcast.33), channel_id=1, source_target_pairs={{0,4},{1,29},{2,6},{3,31},{4,8},{5,1},{6,10},{7,3},{8,12},{9,5},{1... | collective-permute-start | bytes 884744 | tf_op jit(solution)/shard_map/ppermute | solution.py:88
  53.6 10.7 %collective-permute-start.5 = (bf16[192,768]{1,0:T(8,128)(2,1)S(1)}, bf16[192,768]{1,0:T(8,128)(2,1)S(1)}, u32[]{:S(2)}, u32[]{:S(2)}) collective-permute-start(bf16[192,768]{1,0:T(8,128)(2,1)S(1)} %collective-permute-done.3), channel_id=1, source_target_pairs={{0,352},{1,33},{2,354},{3,35},{4,356},{5,37},{6,358},{7,39},{8,360... | collective-permute-start | bytes 884744 | tf_op jit(solution)/shard_map/ppermute | solution.py:91
  56.2 7.8 %collective-permute-start.4 = (bf16[192,768]{1,0:T(8,128)(2,1)S(1)}, bf16[192,768]{1,0:T(8,128)(2,1)S(1)}, u32[]{:S(2)}, u32[]{:S(2)}) collective-permute-start(bf16[192,768]{1,0:T(8,128)(2,1)S(1)} %collective-permute-done.3), channel_id=1, source_target_pairs={{0,4},{1,29},{2,6},{3,31},{4,8},{5,1},{6,10},{7,3},{8,12},{9,5},{1... | collective-permute-start | bytes 884744 | tf_op jit(solution)/shard_map/ppermute | solution.py:91
  58.4 7.8 %collective-permute-start.6 = (bf16[192,768]{1,0:T(8,128)(2,1)S(1)}, bf16[192,768]{1,0:T(8,128)(2,1)S(1)}, u32[]{:S(2)}, u32[]{:S(2)}) collective-permute-start(bf16[192,768]{1,0:T(8,128)(2,1)S(1)} %collective-permute-done.2), channel_id=1, source_target_pairs={{0,384},{1,385},{2,386},{3,387},{4,388},{5,389},{6,390},{7,391},{8... | collective-permute-start | bytes 884744 | tf_op jit(solution)/shard_map/ppermute | solution.py:92
  60.9 5.9 %slice-start = ((s8[9437184]{0:T(1024)(128)(4,1)}), s8[4194304]{0:T(1024)(128)(4,1)S(1)}, s32[]{:S(2)}) async-start(s8[9437184]{0:T(1024)(128)(4,1)} %bitcast.28), calls=%async_computation.1 | async-start | bytes 8388608
  64.0 2.9 %slice-start.1 = ((s8[9437184]{0:T(1024)(128)(4,1)}), s8[4194304]{0:T(1024)(128)(4,1)S(1)}, s32[]{:S(2)}) async-start(s8[9437184]{0:T(1024)(128)(4,1)} %bitcast.28), calls=%async_computation.2 | async-start | bytes 8388608
  66.1 1.2 %slice-start.2 = ((s8[9437184]{0:T(1024)(128)(4,1)}), s8[1048576]{0:T(1024)(128)(4,1)S(1)}, s32[]{:S(2)}) async-start(s8[9437184]{0:T(1024)(128)(4,1)} %bitcast.28), calls=%async_computation.3 | async-start | bytes 2097152
  67.4 8.0 %copy-start = (bf16[2,768,768]{2,1,0:T(8,128)(2,1)S(1)}, bf16[2,768,768]{2,1,0:T(8,128)(2,1)}, u32[]{:S(2)}) copy-start(bf16[2,768,768]{2,1,0:T(8,128)(2,1)} %get-tuple-element.6.refs_0_) | copy-start | bytes 7077892
  69.3 7.9 %collective-permute-start.7 = (bf16[2,256,768]{2,1,0:T(8,128)(2,1)S(1)}, bf16[2,256,768]{2,1,0:T(8,128)(2,1)S(1)}, u32[]{:S(2)}, u32[]{:S(2)}) collective-permute-start(bf16[2,256,768]{2,1,0:T(8,128)(2,1)S(1)} %shard_map.78), channel_id=1, source_target_pairs={{0,1},{1,0},{2,3},{3,2},{4,5},{5,4},{6,7},{7,6},{8,9},{9,8},{10,11... | collective-permute-start | bytes 2359304 | tf_op jit(solution)/shard_map/ppermute | solution.py:111
  76.7 14.3 %copy-start.1 = (f32[256,768]{1,0:T(8,128)S(1)}, f32[256,768]{1,0:T(8,128)}, u32[]{:S(2)}) copy-start(f32[256,768]{1,0:T(8,128)} %param.11) | copy-start | bytes 2359300
  77.3 13.7 %collective-permute-start.8 = (bf16[256,768]{1,0:T(8,128)(2,1)S(1)}, bf16[256,768]{1,0:T(8,128)(2,1)S(1)}, u32[]{:S(2)}, u32[]{:S(2)}) collective-permute-start(bf16[256,768]{1,0:T(8,128)(2,1)S(1)} %fusion.11), channel_id=1, source_target_pairs={{0,2},{2,0},{1,3},{3,1},{4,6},{6,4},{5,7},{7,5},{8,10},{10,8},{9,1... | collective-permute-start | bytes 1179656 | tf_op jit(solution)/shard_map/ppermute | solution.py:114

commit v6 on v5

--- a/solution.py
+++ b/solution.py
@@ -83,13 +83,17 @@
     tables = [
         lax.dynamic_slice_in_dim(couplings, (h * 2 + c) * width, width, 2) for h in (1 - xh, xh)
     ]
-    own, tables = lax.optimization_barrier((own, tables))
+    own, tables[0] = lax.optimization_barrier((own, tables[0]))
     beside = lax.ppermute(own, NAMES, shift(1, 0, 0))
     across = [lax.ppermute(own, NAMES, shift(0, *at)) for at in NEAR]
     pieces = [((0, 0, 0), own)] + [((0,) + at, piece) for at, piece in zip(NEAR, across)]
     pieces += [((1, 0, 0), beside)]
     pieces += [((1,) + at, lax.ppermute(beside, NAMES, shift(0, *at))) for at in NEAR[:2]]
     pieces += [((1,) + NEAR[2], lax.ppermute(across[2], NAMES, shift(1, 0, 0)))]
+
+    at, piece = pieces[-2]
+    piece, tables[1] = lax.optimization_barrier((piece, tables[1]))
+    pieces[-2] = (at, piece)
 
     within = jnp.arange(8, dtype=jnp.int32)
     target = jnp.where(

time: 93.1 us -> 92.7 us (level)
  transfers between devices with their start and end apart: 10 -> 10, of which waited for: 5 -> 6; matrix products, arithmetic and copies ran while one was open for 11% -> 11% of each run, Pallas kernels for 1% -> 2%
where the time goes in v6:
time: 92.7 us; the launch traced here: 91.9 us
  starting transfers between devices  49 us (53%)
  waiting for transfers between devices  24.1 us (26%)
  local copies, waits for them, and re-layouts  7.44 us (8%)
  other arithmetic  3.71 us (4%)
  Pallas kernels  3.36 us (4%)
  matrix products  3.26 us (4%)
  between operations  1.02 us (1%)
    all_to_all x1, starting transfers between devices, shards(): own = lax.all_to_all(spread, FAR, 0, 0, tiled=True).reshape(192, width)  20.6 us
    all_to_all x1, waiting for transfers between devices, shards(): own = lax.all_to_all(spread, FAR, 0, 0, tiled=True).reshape(192, width)  11 us
    ppermute x1, waiting for transfers between devices, shards(): far_in = lax.ppermute(far, 'xh', SWAP)  9.36 us
    ppermute x3, starting transfers between devices, shards(): across = [lax.ppermute(own, NAMES, shift(0, *at)) for at in NEAR]  8.59 us
    ppermute x1, starting transfers between devices, shards(): beside_in = lax.ppermute(out, 'c', SWAP)  5.52 us
    ppermute x2, starting transfers between devices, shards(): lax.ppermute(beside, NAMES, shift(0, *at))  4.69 us
    ppermute x1, starting transfers between devices, shards(): far_in = lax.ppermute(far, 'xh', SWAP)  4.36 us
    dynamic_slice x1, local copies, waits for them, and re-layouts, shards(): lax.dynamic_slice_in_dim(couplings, (h * 2 + c) * width, width, 2)  4.16 us
  transfers between devices with their start and end apart: 10, of which 6 were waited for; matrix products, arithmetic and copies ran while one was open for 11% of the time, Pallas kernels for 2%

profile of v6, /device:TPU:1, one launch (start us, length us, event | category | flops | bytes accessed | tf_op | source)
XLA Modules:
  0.0 91.9 jit_solution(14632523387695564152)
XLA Ops:
  0.6 1.4 %broadcast_in_dim.7 = bf16[24,8,768]{2,1,0:T(8,128)(2,1)} broadcast(bf16[8,768]{1,0:T(8,128)(2,1)} %param.6), dimensions={1,2} | broadcast | bytes 307200 | tf_op jit(solution)/shard_map/broadcast_in_dim | solution.py:81
  2.1 20.6 %all-to-all-start = ((bf16[24,8,768]{2,1,0:T(8,128)(2,1)}), bf16[24,8,768]{2,1,0:T(8,128)(2,1)S(1)}, u32[]{:S(2)}, u32[]{:S(2)}) async-start(bf16[24,8,768]{2,1,0:T(8,128)(2,1)} %broadcast_in_dim.7), calls=%async_computation | async-start | bytes 589824 | tf_op jit(solution)/shard_map/all_to_all | solution.py:82
  22.7 0.5 broadcast.20
  23.2 1.3 %reduce.5 = s32[192]{0:T(256)S(1)} reduce(s32[1,192]{1,0:T(1,128)} %param.9, s32[]{:T(128)} %broadcast.20), dimensions={0}, to_apply=%param.9.reduce_sub_computation.3 | reduce | bytes 1540 | tf_op args[3]
  24.6 0.2 lt.121
  24.7 0.3 copy.8
  25.0 0.7 add_reduce_fusion
  25.8 0.2 add.151
  26.0 0.1 fusion.20
  26.1 0.1 reshape.39
  26.3 4.2 %constant_dynamic-slice_fusion.1 = (bf16[2,768,768]{2,1,0:T(8,128)(2,1)S(1)}, bf16[2,768,768]{2,1,0:T(8,128)(2,1)}) fusion(bf16[2,768,3072]{2,1,0:T(8,128)(2,1)} %table_ref.1, s32[]{:T(128)S(6)} %select_n.124, s32[]{:T(128)S(6)} %select_n.117), kind=kLoop, calls=%fused_computation.37 | loop fusion | bytes 9437192 | tf_op jit(solution)/shard_map/dynamic_slice | solution.py:84
  30.5 11.0 %all-to-all-done = bf16[24,8,768]{2,1,0:T(8,128)(2,1)S(1)} async-done(((bf16[24,8,768]{2,1,0:T(8,128)(2,1)}), bf16[24,8,768]{2,1,0:T(8,128)(2,1)S(1)}, u32[]{:S(2)}, u32[]{:S(2)}) %all-to-all-start) | async-done | bytes 294944 | tf_op jit(solution)/shard_map/all_to_all | solution.py:82
  41.4 3.1 %collective-permute-start.3 = (bf16[192,768]{1,0:T(8,128)(2,1)S(1)}, bf16[192,768]{1,0:T(8,128)(2,1)S(1)}, u32[]{:S(2)}, u32[]{:S(2)}) collective-permute-start(bf16[192,768]{1,0:T(8,128)(2,1)S(1)} %bitcast.30), channel_id=1, source_target_pairs={{0,384},{1,385},{2,386},{3,387},{4,388},{5,389},{6,390},{7,391},{8... | collective-permute-start | bytes 884744 | tf_op jit(solution)/shard_map/ppermute | solution.py:87
  44.6 3.4 %collective-permute-start.2 = (bf16[192,768]{1,0:T(8,128)(2,1)S(1)}, bf16[192,768]{1,0:T(8,128)(2,1)S(1)}, u32[]{:S(2)}, u32[]{:S(2)}) collective-permute-start(bf16[192,768]{1,0:T(8,128)(2,1)S(1)} %bitcast.31), channel_id=1, source_target_pairs={{0,356},{1,61},{2,358},{3,63},{4,360},{5,33},{6,362},{7,35},{8,364... | collective-permute-start | bytes 884744 | tf_op jit(solution)/shard_map/ppermute | solution.py:88
  47.9 0.1 pad_add_fusion.starts
  48.0 3.3 %collective-permute-start.1 = (bf16[192,768]{1,0:T(8,128)(2,1)S(1)}, bf16[192,768]{1,0:T(8,128)(2,1)S(1)}, u32[]{:S(2)}, u32[]{:S(2)}) collective-permute-start(bf16[192,768]{1,0:T(8,128)(2,1)S(1)} %bitcast.32), channel_id=1, source_target_pairs={{0,352},{1,33},{2,354},{3,35},{4,356},{5,37},{6,358},{7,39},{8,360... | collective-permute-start | bytes 884744 | tf_op jit(solution)/shard_map/ppermute | solution.py:88
  51.3 1.9 %collective-permute-start = (bf16[192,768]{1,0:T(8,128)(2,1)S(1)}, bf16[192,768]{1,0:T(8,128)(2,1)S(1)}, u32[]{:S(2)}, u32[]{:S(2)}) collective-permute-start(bf16[192,768]{1,0:T(8,128)(2,1)S(1)} %bitcast.33), channel_id=1, source_target_pairs={{0,4},{1,29},{2,6},{3,31},{4,8},{5,1},{6,10},{7,3},{8,12},{9,5},{1... | collective-permute-start | bytes 884744 | tf_op jit(solution)/shard_map/ppermute | solution.py:88
  53.3 0.4 fusion.3
  53.6 0.0 collective-permute-done.3
  53.6 2.5 %collective-permute-start.5 = (bf16[192,768]{1,0:T(8,128)(2,1)S(1)}, bf16[192,768]{1,0:T(8,128)(2,1)S(1)}, u32[]{:S(2)}, u32[]{:S(2)}) collective-permute-start(bf16[192,768]{1,0:T(8,128)(2,1)S(1)} %collective-permute-done.3), channel_id=1, source_target_pairs={{0,352},{1,33},{2,354},{3,35},{4,356},{5,37},{6,358},{7,39},{8,360... | collective-permute-start | bytes 884744 | tf_op jit(solution)/shard_map/ppermute | solution.py:91
  56.2 2.2 %collective-permute-start.4 = (bf16[192,768]{1,0:T(8,128)(2,1)S(1)}, bf16[192,768]{1,0:T(8,128)(2,1)S(1)}, u32[]{:S(2)}, u32[]{:S(2)}) collective-permute-start(bf16[192,768]{1,0:T(8,128)(2,1)S(1)} %collective-permute-done.3), channel_id=1, source_target_pairs={{0,4},{1,29},{2,6},{3,31},{4,8},{5,1},{6,10},{7,3},{8,12},{9,5},{1... | collective-permute-start | bytes 884744 | tf_op jit(solution)/shard_map/ppermute | solution.py:91
  58.4 0.0 collective-permute-done.2
  58.4 2.2 %collective-permute-start.6 = (bf16[192,768]{1,0:T(8,128)(2,1)S(1)}, bf16[192,768]{1,0:T(8,128)(2,1)S(1)}, u32[]{:S(2)}, u32[]{:S(2)}) collective-permute-start(bf16[192,768]{1,0:T(8,128)(2,1)S(1)} %collective-permute-done.2), channel_id=1, source_target_pairs={{0,384},{1,385},{2,386},{3,387},{4,388},{5,389},{6,390},{7,391},{8... | collective-permute-start | bytes 884744 | tf_op jit(solution)/shard_map/ppermute | solution.py:92
  60.5 0.4 fusion.6
  60.9 0.0 slice-start
  60.9 0.4 fusion.7
  61.3 0.0 collective-permute-done
  61.3 0.4 fusion.4
  61.7 0.0 collective-permute-done.1
  61.7 0.4 fusion.5
  62.1 0.5 collective-permute-done.5
  62.6 0.0 slice-start.1
  62.6 0.4 fusion.9
  63.0 1.0 %collective-permute-done.4 = bf16[192,768]{1,0:T(8,128)(2,1)S(1)} collective-permute-done((bf16[192,768]{1,0:T(8,128)(2,1)S(1)}, bf16[192,768]{1,0:T(8,128)(2,1)S(1)}, u32[]{:S(2)}, u32[]{:S(2)}) %collective-permute-start.4) | collective-permute-done | bytes 294944 | tf_op jit(solution)/shard_map/ppermute | solution.py:91
  64.0 0.4 fusion.8
  64.3 1.8 %collective-permute-done.6 = bf16[192,768]{1,0:T(8,128)(2,1)S(1)} collective-permute-done((bf16[192,768]{1,0:T(8,128)(2,1)S(1)}, bf16[192,768]{1,0:T(8,128)(2,1)S(1)}, u32[]{:S(2)}, u32[]{:S(2)}) %collective-permute-start.6) | collective-permute-done | bytes 294944 | tf_op jit(solution)/shard_map/ppermute | solution.py:92
  66.1 0.0 slice-start.2
  66.1 0.7 add_convert_fusion.rows_ref
  66.8 0.0 slice-done
  66.8 0.0 slice-done.1
  66.8 0.5 slice-done.2
  67.4 0.0 copy-start
  67.4 2.0 %shard_map.78 = bf16[2,256,768]{2,1,0:T(8,128)(2,1)S(1)} custom-call(s32[2]{0:T(128)S(1)} %pad_add_fusion.starts, bf16[512,768]{1,0:T(8,128)(2,1)S(1)} %add_convert_fusion.rows_ref, bf16[2,768,3072]{2,1,0:T(8,128)(2,1)S(1)} %bitcast.29), custom_call_target="tpu_custom_call" | custom-call | flops 1207959552 | bytes 4718592 | tf_op jit(solution)/shard_map/pallas_call | solution.py:61
  69.3 5.5 %collective-permute-start.7 = (bf16[2,256,768]{2,1,0:T(8,128)(2,1)S(1)}, bf16[2,256,768]{2,1,0:T(8,128)(2,1)S(1)}, u32[]{:S(2)}, u32[]{:S(2)}) collective-permute-start(bf16[2,256,768]{2,1,0:T(8,128)(2,1)S(1)} %shard_map.78), channel_id=1, source_target_pairs={{0,1},{1,0},{2,3},{3,2},{4,5},{5,4},{6,7},{7,6},{8,9},{9,8},{10,11... | collective-permute-start | bytes 2359304 | tf_op jit(solution)/shard_map/ppermute | solution.py:115
  74.9 0.0 copy-done
  74.9 1.4 %shard_map.77 = f32[2,256,768]{2,1,0:T(8,128)S(1)} custom-call(bf16[512,768]{1,0:T(8,128)(2,1)S(1)} %add_convert_fusion.rows_ref, bf16[2,768,768]{2,1,0:T(8,128)(2,1)S(1)} %copy-done, bf16[2,768,768]{2,1,0:T(8,128)(2,1)S(1)} %get-tuple-element.9.refs_1_), custom_call_target="tpu_custom_call" | custom-call | flops 1207959552 | bytes 4718592 | tf_op jit(solution)/shard_map/pallas_call | solution.py:61
  76.3 0.0 copy-start.1
  76.3 0.5 collective-permute-done.7
  76.8 0.1 fusion.11
  76.8 4.4 %collective-permute-start.8 = (bf16[256,768]{1,0:T(8,128)(2,1)S(1)}, bf16[256,768]{1,0:T(8,128)(2,1)S(1)}, u32[]{:S(2)}, u32[]{:S(2)}) collective-permute-start(bf16[256,768]{1,0:T(8,128)(2,1)S(1)} %fusion.11), channel_id=1, source_target_pairs={{0,2},{2,0},{1,3},{3,1},{4,6},{6,4},{5,7},{7,5},{8,10},{10,8},{9,1... | collective-permute-start | bytes 1179656 | tf_op jit(solution)/shard_map/ppermute | solution.py:118
  81.2 9.4 %collective-permute-done.8 = bf16[256,768]{1,0:T(8,128)(2,1)S(1)} collective-permute-done((bf16[256,768]{1,0:T(8,128)(2,1)S(1)}, bf16[256,768]{1,0:T(8,128)(2,1)S(1)}, u32[]{:S(2)}, u32[]{:S(2)}) %collective-permute-start.8) | collective-permute-done | bytes 393248 | tf_op jit(solution)/shard_map/ppermute | solution.py:118
  90.6 0.0 copy-done.1
  90.6 1.4 %negate_divide_fusion = (f32[256,768]{1,0:T(8,128)}, f32[256,768]{1,0:T(8,128)}) fusion(f32[256,768]{1,0:T(8,128)S(1)} %copy-done.1, bf16[256,768]{1,0:T(8,128)(2,1)S(1)} %collective-permute-done.8, bf16[2,256,768]{2,1,0:T(8,128)(2,1)S(1)} %collective-permute-done.7, f32[2,256,768]{2,1,0:T(8,128)S(1)} %shard_map.77), kind=kLoop, calls=%fused_computation.6 | loop fusion | flops 1376256 | bytes 3932160 | tf_op jit(solution)/shard_map/div | solution.py:120
  (2 shorter events, 0.0 us)
Async XLA Ops:
  2.1 39.4 %all-to-all-start = ((bf16[24,8,768]{2,1,0:T(8,128)(2,1)}), bf16[24,8,768]{2,1,0:T(8,128)(2,1)S(1)}, u32[]{:S(2)}, u32[]{:S(2)}) async-start(bf16[24,8,768]{2,1,0:T(8,128)(2,1)} %broadcast_in_dim.7), calls=%async_computation | async-start | bytes 589824 | tf_op jit(solution)/shard_map/all_to_all | solution.py:82
  41.4 12.2 %collective-permute-start.3 = (bf16[192,768]{1,0:T(8,128)(2,1)S(1)}, bf16[192,768]{1,0:T(8,128)(2,1)S(1)}, u32[]{:S(2)}, u32[]{:S(2)}) collective-permute-start(bf16[192,768]{1,0:T(8,128)(2,1)S(1)} %bitcast.30), channel_id=1, source_target_pairs={{0,384},{1,385},{2,386},{3,387},{4,388},{5,389},{6,390},{7,391},{8... | collective-permute-start | bytes 884744 | tf_op jit(solution)/shard_map/ppermute | solution.py:87
  44.6 13.8 %collective-permute-start.2 = (bf16[192,768]{1,0:T(8,128)(2,1)S(1)}, bf16[192,768]{1,0:T(8,128)(2,1)S(1)}, u32[]{:S(2)}, u32[]{:S(2)}) collective-permute-start(bf16[192,768]{1,0:T(8,128)(2,1)S(1)} %bitcast.31), channel_id=1, source_target_pairs={{0,356},{1,61},{2,358},{3,63},{4,360},{5,33},{6,362},{7,35},{8,364... | collective-permute-start | bytes 884744 | tf_op jit(solution)/shard_map/ppermute | solution.py:88
  48.0 13.7 %collective-permute-start.1 = (bf16[192,768]{1,0:T(8,128)(2,1)S(1)}, bf16[192,768]{1,0:T(8,128)(2,1)S(1)}, u32[]{:S(2)}, u32[]{:S(2)}) collective-permute-start(bf16[192,768]{1,0:T(8,128)(2,1)S(1)} %bitcast.32), channel_id=1, source_target_pairs={{0,352},{1,33},{2,354},{3,35},{4,356},{5,37},{6,358},{7,39},{8,360... | collective-permute-start | bytes 884744 | tf_op jit(solution)/shard_map/ppermute | solution.py:88
  51.3 10.0 %collective-permute-start = (bf16[192,768]{1,0:T(8,128)(2,1)S(1)}, bf16[192,768]{1,0:T(8,128)(2,1)S(1)}, u32[]{:S(2)}, u32[]{:S(2)}) collective-permute-start(bf16[192,768]{1,0:T(8,128)(2,1)S(1)} %bitcast.33), channel_id=1, source_target_pairs={{0,4},{1,29},{2,6},{3,31},{4,8},{5,1},{6,10},{7,3},{8,12},{9,5},{1... | collective-permute-start | bytes 884744 | tf_op jit(solution)/shard_map/ppermute | solution.py:88
  53.6 9.0 %collective-permute-start.5 = (bf16[192,768]{1,0:T(8,128)(2,1)S(1)}, bf16[192,768]{1,0:T(8,128)(2,1)S(1)}, u32[]{:S(2)}, u32[]{:S(2)}) collective-permute-start(bf16[192,768]{1,0:T(8,128)(2,1)S(1)} %collective-permute-done.3), channel_id=1, source_target_pairs={{0,352},{1,33},{2,354},{3,35},{4,356},{5,37},{6,358},{7,39},{8,360... | collective-permute-start | bytes 884744 | tf_op jit(solution)/shard_map/ppermute | solution.py:91
  56.2 7.8 %collective-permute-start.4 = (bf16[192,768]{1,0:T(8,128)(2,1)S(1)}, bf16[192,768]{1,0:T(8,128)(2,1)S(1)}, u32[]{:S(2)}, u32[]{:S(2)}) collective-permute-start(bf16[192,768]{1,0:T(8,128)(2,1)S(1)} %collective-permute-done.3), channel_id=1, source_target_pairs={{0,4},{1,29},{2,6},{3,31},{4,8},{5,1},{6,10},{7,3},{8,12},{9,5},{1... | collective-permute-start | bytes 884744 | tf_op jit(solution)/shard_map/ppermute | solution.py:91
  58.4 7.8 %collective-permute-start.6 = (bf16[192,768]{1,0:T(8,128)(2,1)S(1)}, bf16[192,768]{1,0:T(8,128)(2,1)S(1)}, u32[]{:S(2)}, u32[]{:S(2)}) collective-permute-start(bf16[192,768]{1,0:T(8,128)(2,1)S(1)} %collective-permute-done.2), channel_id=1, source_target_pairs={{0,384},{1,385},{2,386},{3,387},{4,388},{5,389},{6,390},{7,391},{8... | collective-permute-start | bytes 884744 | tf_op jit(solution)/shard_map/ppermute | solution.py:92
  60.9 5.9 %slice-start = ((s8[9437184]{0:T(1024)(128)(4,1)}), s8[4194304]{0:T(1024)(128)(4,1)S(1)}, s32[]{:S(2)}) async-start(s8[9437184]{0:T(1024)(128)(4,1)} %bitcast.28), calls=%async_computation.1 | async-start | bytes 8388608
  62.6 4.2 %slice-start.1 = ((s8[9437184]{0:T(1024)(128)(4,1)}), s8[4194304]{0:T(1024)(128)(4,1)S(1)}, s32[]{:S(2)}) async-start(s8[9437184]{0:T(1024)(128)(4,1)} %bitcast.28), calls=%async_computation.2 | async-start | bytes 8388608
  66.1 1.2 %slice-start.2 = ((s8[9437184]{0:T(1024)(128)(4,1)}), s8[1048576]{0:T(1024)(128)(4,1)S(1)}, s32[]{:S(2)}) async-start(s8[9437184]{0:T(1024)(128)(4,1)} %bitcast.28), calls=%async_computation.3 | async-start | bytes 2097152
  67.4 7.5 %copy-start = (bf16[2,768,768]{2,1,0:T(8,128)(2,1)S(1)}, bf16[2,768,768]{2,1,0:T(8,128)(2,1)}, u32[]{:S(2)}) copy-start(bf16[2,768,768]{2,1,0:T(8,128)(2,1)} %get-tuple-element.8.refs_0_) | copy-start | bytes 7077892
  69.3 7.4 %collective-permute-start.7 = (bf16[2,256,768]{2,1,0:T(8,128)(2,1)S(1)}, bf16[2,256,768]{2,1,0:T(8,128)(2,1)S(1)}, u32[]{:S(2)}, u32[]{:S(2)}) collective-permute-start(bf16[2,256,768]{2,1,0:T(8,128)(2,1)S(1)} %shard_map.78), channel_id=1, source_target_pairs={{0,1},{1,0},{2,3},{3,2},{4,5},{5,4},{6,7},{7,6},{8,9},{9,8},{10,11... | collective-permute-start | bytes 2359304 | tf_op jit(solution)/shard_map/ppermute | solution.py:115
  76.3 14.3 %copy-start.1 = (f32[256,768]{1,0:T(8,128)S(1)}, f32[256,768]{1,0:T(8,128)}, u32[]{:S(2)}) copy-start(f32[256,768]{1,0:T(8,128)} %param.11) | copy-start | bytes 2359300
  76.8 13.7 %collective-permute-start.8 = (bf16[256,768]{1,0:T(8,128)(2,1)S(1)}, bf16[256,768]{1,0:T(8,128)(2,1)S(1)}, u32[]{:S(2)}, u32[]{:S(2)}) collective-permute-start(bf16[256,768]{1,0:T(8,128)(2,1)S(1)} %fusion.11), channel_id=1, source_target_pairs={{0,2},{2,0},{1,3},{3,1},{4,6},{6,4},{5,7},{7,5},{8,10},{10,8},{9,1... | collective-permute-start | bytes 1179656 | tf_op jit(solution)/shard_map/ppermute | solution.py:118
